TPU v7x, 128 devices: a whole 4x4x4 slice. The times are simulated.
128 devices in a mesh: lat: 8 (over y, core), wave: 16 (over z, x).
Axes of the slice: x: 4, y: 4, z: 4, core: 2. Of those that a mesh axis runs over, the one named last changes fastest.
Arguments:
- grid_field: bfloat16 [2, 512, 64, 2048], P(None, 'lat', 'wave'), may hold values from -6 to 6
- points: int32 [512], P('lat'), may hold values from 16 to 2048, as said below
- weights: float32 [512], P('lat'), may hold values from 0.5 to 2
- owners: int32 [256], replicated, may hold values from 0 to 255, as said below
- legendre: bfloat16 [256, 2, 512, 512], P('wave'), may hold values from -0.0805 to 0.0805, as said below
- spectral_variance: float32 [64, 1024], P('lat'), may hold values from 0.1 to 1
- vertical: bfloat16 [64, 64], replicated, may hold values from -0.305 to 1.81
Outputs:
- smoothed: bfloat16 [2, 512, 64, 2048], P(None, 'lat', 'wave')
Inputs may be any that keep to these rules, and one draw needn't show every extreme that they name: `owners`: every wavenumber appears once. Owner w along wave holds slots w * 16 to (w+1) * 16 - 1; slots 2t and 2t+1 hold m and 255 - m. Never falling from the pole toward the equator; the row nearest the equator has exactly 2048 points. legendre[r, q, k, i] is zero where 2k+q < owners[r].
All inputs are finite; a program needn't handle non-finite values.
Results may differ from a plain program's by a relative error of at most 0.014.
Values may be sent and summed in bfloat16 or wider, within the bound.
No kernel may reach another device: no remote copies, remote signals or barrier semaphores. Data moves between devices by JAX's collectives and lax.ppermute only.
A program may use at most 192 MiB of HBM per device.

v0:
```python
import math

import jax
import jax.numpy as jnp
from jax import lax
from jax.sharding import PartitionSpec as P


def fourier_factors(row_points, owners, column_start, width):
    column_index = column_start + jnp.arange(width, dtype=jnp.int32)
    phase_index = owners[None, :] * column_index[:, None] % row_points
    angles = phase_index.astype(jnp.float32) * (2.0 * math.pi) / row_points.astype(jnp.float32)
    inside = (column_index[:, None] < row_points) & (2 * owners[None, :] < row_points)
    inside = jnp.concatenate([inside, inside], axis=1)
    factors = jnp.concatenate([jnp.cos(angles), -jnp.sin(angles)], axis=1)
    return jnp.where(inside, factors, 0.0).astype(jnp.bfloat16)


def local(grid_field, points, weights, owners, legendre, spectral_variance, vertical):
    band_rows = grid_field.shape[1]
    longitudes = grid_field.shape[3]
    slot_count = owners.shape[0]
    levels = vertical.shape[0]
    wave_index = lax.axis_index("wave")
    wave_count = lax.axis_size("wave")
    few_rows = band_rows // wave_count
    row_start = wave_index * few_rows
    local_points = lax.dynamic_slice_in_dim(points, row_start, few_rows, 0)
    regrouped = lax.all_to_all(grid_field, "wave", split_axis=3, concat_axis=2, tiled=True)
    block_width = regrouped.shape[3]
    column_start = wave_index * block_width

    def partial_sums(row_index):
        row_points = points[row_index]
        factors = fourier_factors(row_points, owners, column_start, block_width)
        row_values = lax.dynamic_index_in_dim(regrouped, row_index, 1, keepdims=False)
        spectrum = jnp.dot(
            row_values.reshape(2 * levels, block_width), factors, preferred_element_type=jnp.float32
        )
        spectrum = spectrum * (weights[row_index] / row_points.astype(jnp.float32))
        return spectrum.reshape(2, levels, 2, slot_count)

    partials = lax.map(partial_sums, jnp.arange(band_rows, dtype=jnp.int32))
    summed = lax.psum_scatter(partials, "wave", scatter_dimension=4, tiled=True)
    folded = jnp.stack([summed[:, 0] + summed[:, 1], summed[:, 0] - summed[:, 1]], axis=1)
    folded = jnp.transpose(folded, (4, 1, 3, 2, 0)).astype(jnp.bfloat16)
    arrived = jnp.einsum(
        "msclh,lo->mscoh", folded, vertical, preferred_element_type=jnp.float32
    ).astype(jnp.bfloat16)
    at_owners = lax.all_to_all(arrived, "lat", split_axis=3, concat_axis=4, tiled=True)
    own_slots = at_owners.shape[0]
    levels_spec = at_owners.shape[3]
    lat_count = at_owners.shape[4]
    own_waves = lax.dynamic_slice_in_dim(owners, wave_index * own_slots, own_slots, 0)
    parity = (own_waves % 2)[:, None, None]
    paired = at_owners.reshape(own_slots, 2, 2 * levels_spec, lat_count)
    even_rows = jnp.where(parity == 0, paired[:, 0], paired[:, 1])
    odd_rows = jnp.where(parity == 1, paired[:, 0], paired[:, 1])
    operand = jnp.stack([even_rows, odd_rows], axis=1)
    coefficient = jnp.einsum(
        "mqkl,mqcl->mqck", legendre, operand, preferred_element_type=jnp.float32
    )
    half_degree = coefficient.shape[3]
    spread = spectral_variance.reshape(levels_spec, half_degree, 2).transpose(2, 0, 1)
    scaled = (
        coefficient.reshape(own_slots, 2, 2, levels_spec, half_degree) * spread[None, :, None, :, :]
    )
    scaled = scaled.astype(jnp.bfloat16).reshape(own_slots, 2, 2 * levels_spec, half_degree)
    synthesis = jnp.einsum("mqkl,mqck->mqcl", legendre, scaled, preferred_element_type=jnp.float32)
    symmetric = jnp.where(parity == 0, synthesis[:, 0], synthesis[:, 1])
    antisym = jnp.where(parity == 0, synthesis[:, 1], synthesis[:, 0])
    returned = (
        jnp.stack([symmetric, antisym], axis=1)
        .reshape(own_slots, 2, 2, levels_spec, lat_count)
        .astype(jnp.bfloat16)
    )
    rows_back = lax.all_to_all(returned, "lat", split_axis=4, concat_axis=3, tiled=True)
    remixed = jnp.einsum(
        "msclh,ol->mscoh", rows_back, vertical, preferred_element_type=jnp.float32
    ).astype(jnp.bfloat16)
    gathered = lax.all_to_all(remixed, "wave", split_axis=4, concat_axis=0, tiled=True)
    gathered = gathered.astype(jnp.float32)
    unfolded = jnp.stack(
        [gathered[:, 0] + gathered[:, 1], gathered[:, 0] - gathered[:, 1]], axis=0
    ).astype(jnp.bfloat16)
    per_row = jnp.transpose(unfolded, (4, 0, 3, 2, 1))
    doubling = jnp.where(owners == 0, 1.0, 2.0).astype(jnp.bfloat16)
    doubling = jnp.concatenate([doubling, doubling])

    def synthesise(row_index):
        row_points = local_points[row_index]
        factors = fourier_factors(row_points, owners, 0, longitudes) * doubling
        coefs_row = lax.dynamic_index_in_dim(per_row, row_index, 0, keepdims=False)
        coefs_row = coefs_row.reshape(2 * levels, 2 * slot_count)
        gridded = jnp.einsum("cm,jm->cj", coefs_row, factors, preferred_element_type=jnp.float32)
        return gridded.reshape(2, levels, longitudes).astype(jnp.bfloat16)

    result_rows = lax.map(synthesise, jnp.arange(few_rows, dtype=jnp.int32))
    result_rows = jnp.transpose(result_rows, (1, 0, 2, 3))
    return lax.all_to_all(result_rows, "wave", split_axis=2, concat_axis=1, tiled=True)


def solution(mesh):
    return jax.shard_map(
        local,
        mesh=mesh,
        in_specs=(
            P(None, "lat", "wave", None),
            P("lat"),
            P("lat"),
            P(),
            P("wave", None, None, None),
            P("lat", None),
            P(),
        ),
        out_specs=P(None, "lat", "wave", None),
        check_vma=False,
    )
```

profile of v0, /device:TPU:1, one launch (start us, length us, event | category | flops | bytes accessed | tf_op | source)
XLA Modules:
  0.0 1265.9 jit_solution(8335285682298510480)
XLA Ops:
  6.5 7.5 copy.76
  14.1 7.5 reshape.107
  21.6 8.4 all-to-all-start
  30.1 30.4 %all-to-all-done = bf16[16,2,32768]{2,1,0:T(2,128)(2,1)S(1)} async-done(((bf16[16,2,32768]{2,1,0:T(2,128)(2,1)}), bf16[16,2,32768]{2,1,0:T(2,128)(2,1)S(1)}, u32[]{:S(2)}, u32[]{:S(2)}) %all-to-all-start) | async-done | bytes 2097184 | tf_op jit(solution)/shard_map/all_to_all | solution.py:29
  60.5 5.0 reshape.108
  65.5 6.4 copy.77
  72.0 685.8 %while.20 = (s32[]{:T(128)}, f32[64,2,64,2,256]{4,3,2,1,0:T(2,128)}, s32[64]{0:T(128)S(1)}, bf16[2,64,64,128]{3,2,1,0:T(8,128)(2,1)S(1)}, s32[]{:T(128)}, /*inde...) while((s32[]{:T(128)}, ...), condition=%wide.region_1.2_spmd, body=%wide.region_0.1_spmd.sunk | while | flops 17728392 | bytes 1741319 | solution.py:43
  87.8 1.9 fusion.70
  98.5 1.9 fusion.70
  109.2 1.9 fusion.70
  120.0 1.9 fusion.70
  130.7 1.9 fusion.70
  152.1 1.9 fusion.70
  162.8 1.9 fusion.70
  173.5 1.9 fusion.70
  184.2 1.9 fusion.70
  194.9 1.9 fusion.70
  205.6 1.9 fusion.70
  216.3 1.9 fusion.70
  227.1 1.9 fusion.70
  237.8 1.9 fusion.70
  280.6 1.9 fusion.70
  291.4 1.9 fusion.70
  302.1 1.9 fusion.70
  312.8 1.9 fusion.70
  334.2 1.9 fusion.70
  344.9 1.9 fusion.70
  757.8 31.2 %copy.78 = f32[64,2,64,2,256]{2,0,3,1,4:T(8,128)} copy(f32[64,2,64,2,256]{4,3,2,1,0:T(2,128)} %get-tuple-element.84) | data formatting | bytes 33554432 | tf_op jit(solution)/shard_map/while | solution.py:43
  789.0 194.5 %reduce-scatter.2.cloned.1.call-done = f32[64,2,64,2,16]{2,0,3,1,4:T(8,128)} async-done(((f32[64,2,64,2,256]{2,0,3,1,4:T(8,128)}), f32[64,2,64,2,16]{2,0,3,1,4:T(8,128)}) %reduce-scatter.2.cloned.1.call-update) | async-done | bytes 1048592 | tf_op jit(solution)/shard_map/reduce_scatter | solution.py:44
  988.4 5.3 all-to-all-start.1
  994.2 9.0 all-to-all-done.1
  1006.1 14.0 %fusion.37 = bf16[16,2,16,512]{3,2,1,0:T(8,128)(2,1)S(1)} fusion(bf16[16,2,512,512]{3,2,1,0:T(8,128)(2,1)} %param.15, bf16[16,1,16,512]{3,2,1,0:T(8,128)(2,1)S(1)} %get-tuple-element.164, bf16[16,1,16,512]{3,2,1,0:T(8,128)(2,1)S(1)} %get-tuple-element.163, f32[2,16,512]{2,1,0:T(8,128)S(1)} %broadcast_bitcast_fusion), kind=kOutput, calls=%fused_computation.67 | convolution fusion | flops 537657344 | bytes 17891328 | tf_op jit(solution)/shard_map/mqkl,mqck->mqcl/dot_general | solution.py:69
  1020.2 2.1 copy.84
  1022.3 2.9 copy.85
  1025.2 4.3 fusion.56
  1029.5 5.7 reshape.111
  1035.3 12.6 all_to_all.78
  1047.9 4.1 reshape.112
  1052.0 5.2 copy.87
  1060.2 4.6 all-to-all-start.3
  1065.0 10.2 all-to-all-done.3
  1077.1 148.1 %while.21 = (s32[]{:T(128)}, bf16[4,2,64,2048]{3,1,0,2:T(2,128)(2,1)}, s32[4]{0:T(128)S(1)}, bf16[4,2,64,2,256]{4,3,2,1,0:T(2,128)(2,1)S(1)}, s32[4]{0:T(128)S(1...) while((s32[]{:T(128)}, bf16[4,2,64,2048]{3,1,0,2:T(2,128)(2,1)}, ...), condition=%wide.region_4.5_spmd, body=%wide.region_3.4_spmd.sunk | while | flops 287050240 | bytes 7479515 | solution.py:98
  1081.7 28.3 %fusion.73 = (bf16[2048,256]{1,0:T(8,128)(2,1)S(1)}, bf16[2048,256]{1,0:T(8,128)(2,1)S(1)}) fusion(f32[]{:T(128)S(6)} %convert_element_type.121, pred[]{:T(512)S(6)} %lt.153, s32[]{:T(128)S(6)} %select_n.140, s32[256]{0:T(256)S(1)} %get-tuple-element.323), kind=kLoop, calls=%fused_computation.41.clone.1 | loop fusion | flops 7340032 | bytes 2098185 | tf_op jit(solution)/shard_map/while/body/eval_jaxpr/cos | solution.py:15
  1118.7 28.3 %fusion.73 = (bf16[2048,256]{1,0:T(8,128)(2,1)S(1)}, bf16[2048,256]{1,0:T(8,128)(2,1)S(1)}) fusion(f32[]{:T(128)S(6)} %convert_element_type.121, pred[]{:T(512)S(6)} %lt.153, s32[]{:T(128)S(6)} %select_n.140, s32[256]{0:T(256)S(1)} %get-tuple-element.323), kind=kLoop, calls=%fused_computation.41.clone.1 | loop fusion | flops 7340032 | bytes 2098185 | tf_op jit(solution)/shard_map/while/body/eval_jaxpr/cos | solution.py:15
  1155.7 28.3 %fusion.73 = (bf16[2048,256]{1,0:T(8,128)(2,1)S(1)}, bf16[2048,256]{1,0:T(8,128)(2,1)S(1)}) fusion(f32[]{:T(128)S(6)} %convert_element_type.121, pred[]{:T(512)S(6)} %lt.153, s32[]{:T(128)S(6)} %select_n.140, s32[256]{0:T(256)S(1)} %get-tuple-element.323), kind=kLoop, calls=%fused_computation.41.clone.1 | loop fusion | flops 7340032 | bytes 2098185 | tf_op jit(solution)/shard_map/while/body/eval_jaxpr/cos | solution.py:15
  1192.8 28.3 %fusion.73 = (bf16[2048,256]{1,0:T(8,128)(2,1)S(1)}, bf16[2048,256]{1,0:T(8,128)(2,1)S(1)}) fusion(f32[]{:T(128)S(6)} %convert_element_type.121, pred[]{:T(512)S(6)} %lt.153, s32[]{:T(128)S(6)} %select_n.140, s32[256]{0:T(256)S(1)} %get-tuple-element.323), kind=kLoop, calls=%fused_computation.41.clone.1 | loop fusion | flops 7340032 | bytes 2098185 | tf_op jit(solution)/shard_map/while/body/eval_jaxpr/cos | solution.py:15
  1225.2 30.8 %all_to_all.79 = bf16[2,4,64,2048]{3,0,1,2:T(2,128)(2,1)S(1)} all-to-all(bf16[2,4,64,2048]{3,0,1,2:T(2,128)(2,1)} %bitcast.34), channel_id=1, replica_groups=mesh['lat'=8,'wave'=16] {'wave'}, dimensions={2} | all-to-all | bytes 4194304 | tf_op jit(solution)/shard_map/all_to_all | solution.py:100
  1256.0 3.0 copy.93
  (826 shorter events, 388.4 us)
Async XLA Ops:
  6.5 978.8 %copy-start = (bf16[64,64]{1,0:T(8,128)(2,1)S(1)}, bf16[64,64]{1,0:T(8,128)(2,1)}, u32[]{:S(2)}) copy-start(bf16[64,64]{1,0:T(8,128)(2,1)} %param.17) | copy-start | bytes 24580
  21.6 38.9 %all-to-all-start = ((bf16[16,2,32768]{2,1,0:T(2,128)(2,1)}), bf16[16,2,32768]{2,1,0:T(2,128)(2,1)S(1)}, u32[]{:S(2)}, u32[]{:S(2)}) async-start(bf16[16,2,32768]{2,1,0:T(2,128)(2,1)} %reshape.107), calls=%async_computation | async-start | bytes 4194304 | tf_op jit(solution)/shard_map/all_to_all | solution.py:29
  30.0 953.5 %reduce-scatter.2.cloned.1.call-start = ((), (), s32[]{:S(2)}) async-start(), calls=%async_computation.6 | async-start | bytes 35651584 | tf_op jit(solution)/shard_map/reduce_scatter | solution.py:44
  65.5 6.5 copy-start.1
  65.5 6.5 copy-start.3
  65.5 6.5 copy-start.4
  985.8 8.0 copy-start.2
  988.4 14.8 %all-to-all-start.1 = ((bf16[8,2,16384]{2,1,0:T(2,128)(2,1)}), bf16[8,2,16384]{2,1,0:T(2,128)(2,1)S(1)}, u32[]{:S(2)}, u32[]{:S(2)}) async-start(bf16[8,2,16384]{2,1,0:T(2,128)(2,1)} %reshape.109), calls=%async_computation.2 | async-start | bytes 1048576 | tf_op jit(solution)/shard_map/all_to_all | solution.py:50
  1060.2 14.9 %all-to-all-start.3 = ((bf16[16,2,8192]{2,1,0:T(2,128)(2,1)}), bf16[16,2,8192]{2,1,0:T(2,128)(2,1)S(1)}, u32[]{:S(2)}, u32[]{:S(2)}) async-start(bf16[16,2,8192]{2,1,0:T(2,128)(2,1)} %reshape.113), calls=%async_computation.4 | async-start | bytes 1048576 | tf_op jit(solution)/shard_map/all_to_all | solution.py:81
Sparse Core Ops, SparseCore 0:
  789.2 194.3 reduce-scatter.1
where the time goes:
time: 1270 us
  other arithmetic  335 us (26%)
  loops' own time  309 us (24%)
  local copies, waits for them, and re-layouts  272 us (21%)
  waiting for transfers between devices  244 us (19%)
  blocking collectives  43.4 us (3%)
  matrix products  30.4 us (2%)
  starting transfers between devices  18.4 us (1%)
  between operations  13.7 us (1%)
    another operation x1, loops' own time, local(): partials = lax.map(partial_sums, jnp.arange(band_rows, dtype=jnp.int32))  295 us
    cos x68, other arithmetic, fourier_factors(): factors = jnp.concatenate([jnp.cos(angles), -jnp.sin(angles)], axis=1)  232 us
    reduce_scatter x1, waiting for transfers between devices, local(): summed = lax.psum_scatter(partials, 'wave', scatter_dimension=4, tiled=True)  194 us
    dynamic_update_slice x64, local copies, waits for them, and re-layouts, local(): partials = lax.map(partial_sums, jnp.arange(band_rows, dtype=jnp.int32))  46.7 us
    lt x68, other arithmetic, fourier_factors(): column_index[:, None] < row_points  44.2 us
    lt x68, other arithmetic, fourier_factors(): 2 * owners[None, :] < row_points  44.1 us
    dynamic_slice x64, local copies, waits for them, and re-layouts, partial_sums(): spectrum = spectrum * (weights[row_index] / row_points.astype(jnp.float32))  37.7 us
    dynamic_slice x64, local copies, waits for them, and re-layouts, partial_sums(): row_points = points[row_index]  37.6 us
  transfers between devices with their start and end apart: 4, of which 4 were waited for; matrix products, arithmetic and copies ran while one was open for 0% of the time, Pallas kernels for 0%

commit v1 on v0

v1 whole, which is shorter than its diff:
```python
import functools

import jax
import jax.numpy as jnp
import numpy as np
from jax import lax
from jax.experimental import pallas as pl
from jax.experimental.pallas import tpu as pltpu
from jax.sharding import PartitionSpec as P

ROWS = 8
CHUNK = 128
BUILT = 3
VMEM_LIMIT = 56 * 1024 * 1024

SIN_TERMS = (3.141592640130707, -5.167710083507862, 2.550077523214134, -0.5982912856178576, 0.0776576603009221)
COS_TERMS = (0.9999999532476082, -4.93479283061961, 4.058411352862034, -1.3318765680776314, 0.2196896110917421)


def polynomial(terms, square):
    total = jnp.full_like(square, terms[-1])
    for term in terms[-2::-1]:
        total = total * square + term
    return total


def phasor(product, length, inverse):
    turns = jnp.floor(product * inverse + 0.5)
    part = (product - turns * length) * inverse
    square = part * part
    sine = part * polynomial(SIN_TERMS, square)
    cosine = polynomial(COS_TERMS, square)
    return 1.0 - 2.0 * sine * sine, 2.0 * sine * cosine


def multiply(a, b):
    return a[0] * b[0] - a[1] * b[1], a[0] * b[1] + a[1] * b[0]


def square(a):
    return a[0] * a[0] - a[1] * a[1], 2.0 * a[0] * a[1]


def times_transposed(a, b):
    return lax.dot_general(a, b, (((1,), (1,)), ((), ())), preferred_element_type=jnp.float32)


def lengths_by_row(points_ref, first, shape):
    row = lax.broadcasted_iota(jnp.int32, shape, 0)
    lengths = jnp.zeros(shape, jnp.int32)
    for r in range(ROWS):
        lengths = jnp.where(row == r, points_ref[first + r], lengths)
    lengths = lengths.astype(jnp.float32)
    return lengths, 1.0 / lengths


def place_phasors(step_ref, waves, lengths, inverse):
    cosine, sine = phasor(waves, lengths, inverse)
    turn, at = (cosine, -sine), 1
    keep = {1: 0, 2: 2, 4: 4, 8: 6, CHUNK: 10, 2 * CHUNK: 12}
    while True:
        if at in keep:
            step_ref[keep[at]], step_ref[keep[at] + 1] = turn
        if at in (8, 16, 2 * CHUNK):
            step_ref[{8: 8, 16: 9, 2 * CHUNK: 14}[at]] = 2.0 * turn[0]
        if at == 2 * CHUNK:
            break
        turn, at = square(turn), 2 * at


def swap_sublanes(values):
    values = list(values)
    sublane = lax.broadcasted_iota(jnp.int32, values[0].shape, 0)
    for d in (4, 2, 1):
        low = sublane & d == 0
        for a in range(8):
            if a & d == 0:
                first, second = values[a], values[a + d]
                values[a] = jnp.where(low, first, pltpu.roll(second, d, 0))
                values[a + d] = jnp.where(low, pltpu.roll(first, 8 - d, 0), second)
    return values


def steps_of(step_ref, which, r):
    slots = step_ref.shape[2]
    return tuple(jnp.broadcast_to(step_ref[n, r:r + 1, :], (8, slots)) for n in which)


def build_table(table_ref, step_ref, r):
    slots = step_ref.shape[2]
    size = table_ref.shape[0]
    sublane = lax.broadcasted_iota(jnp.int32, (8, slots), 0)
    powers = []
    for n in range(3):
        power = steps_of(step_ref, (2 * n, 2 * n + 1), r)
        powers.append(tuple(jnp.where(sublane & (1 << n) == 0, 1.0 - c, power[c]) for c in range(2)))
    real, imaginary, twice, twice_next = steps_of(step_ref, (6, 7, 8, 9), r)
    values = [multiply(multiply(powers[0], powers[1]), powers[2])]
    values.append(multiply(values[0], (real, imaginary)))
    for n in range(2, size // 8):
        if n < 4:
            values.append(tuple(twice * values[n - 1][c] - values[n - 2][c] for c in range(2)))
        else:
            values.append(tuple(twice_next * values[n - 2][c] - values[n - 4][c] for c in range(2)))
        if n % 2:
            for c in range(2):
                both = jnp.concatenate([values[n - 1][c], values[n][c]], axis=0).astype(jnp.bfloat16)
                table_ref[8 * n - 8:8 * n + 8, c * slots:(c + 1) * slots] = both
        elif n == 2:
            for c in range(2):
                both = jnp.concatenate([values[0][c], values[1][c]], axis=0).astype(jnp.bfloat16)
                table_ref[:16, c * slots:(c + 1) * slots] = both


def analysis_kernel(order, points_ref, weights_ref, wave_ref, owners_ref, variance_ref, field_ref, out_ref,
                    phasors_ref, own_ref, step_ref, table_ref, rows_ref, sums_ref, order_ref, sems, phasor_sems):
    slots = owners_ref.shape[1]
    tiles = [slice(t, t + 128) for t in range(0, slots, 128)]
    rows, height = own_ref.shape[1:3]

    def arrival(g):
        at = pl.ds(g * ROWS, ROWS)
        return pltpu.make_async_copy(field_ref.at[:, at], own_ref.at[:, at], sems.at[g])

    def departure(g):
        at = pl.ds(pl.multiple_of(g * ROWS, ROWS), ROWS)
        return pltpu.make_async_copy(step_ref.at[:, at], phasors_ref.at[:, at], phasor_sems.at[g])

    for g in range(rows // ROWS):
        arrival(g).start()
    waves = jnp.broadcast_to(owners_ref[...].astype(jnp.float32), (ROWS, slots))
    sublane = lax.broadcasted_iota(jnp.int32, (8, slots), 0)
    position = lax.broadcasted_iota(jnp.int32, (height, CHUNK), 0) // 4 * CHUNK
    position = position + lax.broadcasted_iota(jnp.int32, (height, CHUNK), 1)

    def group(g, _):
        first = g * ROWS
        lengths, inverse = lengths_by_row(points_ref, first, (ROWS, slots))
        here = step_ref.at[:, pl.ds(pl.multiple_of(first, ROWS), ROWS)]
        place_phasors(here, waves, lengths, inverse)
        departure(g).start()
        arrival(g).wait()
        for r in range(ROWS):
            length = points_ref[first + r]

            build_table(table_ref.at[r], here, r)
            inside = jnp.where(position < length, 1.0, 0.0).astype(jnp.bfloat16)
            points = jnp.concatenate([own_ref[0, first + r] * inside, own_ref[1, first + r] * inside], axis=0)
            parts = jnp.dot(points, table_ref[r], preferred_element_type=jnp.float32)
            chunk, pair, twice = steps_of(here, (10, 11), r), steps_of(here, (12, 13), r), steps_of(here, (14,), r)[0]
            sums = []
            for h in range(2):
                blocks = [
                    tuple(parts[b:b + 8, c * slots:(c + 1) * slots] for c in range(2))
                    for b in range(h * height, (h + 1) * height, 8)
                ]
                later, total = blocks[-1], tuple(blocks[-2][c] + twice * blocks[-1][c] for c in range(2))
                for part in blocks[-3:0:-1]:
                    later, total = total, tuple(part[c] + (twice * total[c] - later[c]) for c in range(2))
                total = multiply(total, pair)
                sums.append(tuple(total[c] + (blocks[0][c] - later[c]) for c in range(2)))
            scale = weights_ref[first + r] / length.astype(jnp.float32)
            scale = jnp.where(2 * owners_ref[...] < length, scale, 0.0)
            firsts, seconds = [], []
            for c in range(2):
                added, taken = sums[0][c] + sums[1][c], sums[0][c] - sums[1][c]
                firsts.append(jnp.where(sublane < 4, added, pltpu.roll(taken, 4, 0)))
                seconds.append(jnp.where(sublane < 4, pltpu.roll(added, 4, 0), taken))
            seconds = multiply(seconds, chunk)
            for c in range(2):
                rows_ref[c, r] = (firsts[c] + seconds[c]) * scale
        for c in range(2):
            for t, lanes in enumerate(tiles):
                for row, part in enumerate(swap_sublanes([rows_ref[c, r, :, lanes] for r in range(ROWS)])):
                    sums_ref[t, row, pl.ds(pl.multiple_of(c * 64 + first, 8), 8), :] = part
        return 0

    lax.fori_loop(0, rows // ROWS, group, 0)

    for row in range(8):
        for t in range(len(tiles)):
            order_ref[t, row] = sums_ref[t, row].T
    variance = variance_ref[...]
    variance = jnp.where(wave_ref[0] % 2 == 1, pltpu.roll(variance, 64, 1), variance)
    upper = variance.astype(jnp.bfloat16).astype(jnp.float32)
    lane = lax.broadcasted_iota(jnp.int32, variance.shape, 1)
    variance = jnp.where(lane < 64, upper, pltpu.roll(variance - upper, 64, 1)).astype(jnp.bfloat16)
    where = {t: n for n, t in enumerate(order)}
    for slot in range(0, slots, 8):
        at = slice(slot % 128, slot % 128 + 8)
        parts = swap_sublanes([order_ref[slot // 128, row, at, :] for row in range(8)])
        for n in range(0, 8, 2):
            to = where[(slot + n) // 2]
            out_ref[to, :16] = jnp.concatenate(parts[n:n + 2], axis=0).astype(jnp.bfloat16)
            out_ref[to, 16:] = variance
    for g in range(rows // ROWS):
        departure(g).wait()


def matrices_of(made_ref):
    size = made_ref.shape[1]
    return made_ref.at[:size], made_ref.at[size:2 * size], made_ref.at[2 * size:]


def place_matrices(vertical_ref, mix_in_ref, mix_out_ref, parting_ref):
    levels = vertical_ref.shape[0]
    vertical = vertical_ref[...].astype(jnp.float32)
    index = lax.broadcasted_iota(jnp.int32, (4 * levels, levels), 0)
    level = lax.broadcasted_iota(jnp.int32, (4 * levels, levels), 1)
    by_block = jnp.where(level == index // 16 * 4 + index % 4, 1.0, 0.0)
    by_slot = jnp.where(level == index % levels, 1.0, 0.0)
    row = lax.broadcasted_iota(jnp.int32, (4 * levels, 4 * levels), 0)
    col = lax.broadcasted_iota(jnp.int32, (4 * levels, 4 * levels), 1)
    by_rows = jnp.dot(by_block, vertical, preferred_element_type=jnp.float32)
    mix_in = times_transposed(by_slot, by_rows)
    mix_in_ref[...] = jnp.where(row // levels == col % 16 // 4, mix_in, 0.0).astype(jnp.bfloat16)
    mix_out = times_transposed(by_rows, by_slot)
    sign = jnp.where((row % 8 // 4 == 1) & (col // levels % 2 == 1), -1.0, 1.0)
    mix_out_ref[...] = jnp.where(row % 16 // 8 == col // (2 * levels), mix_out * sign, 0.0).astype(jnp.bfloat16)
    degree = lax.broadcasted_iota(jnp.int32, parting_ref.shape, 0)
    degree = degree // 128 * 64 + degree % 64
    lane = lax.broadcasted_iota(jnp.int32, parting_ref.shape, 1)
    parting_ref[...] = jnp.where(degree == 2 * (lane % 128) + lane // 128, 1.0, 0.0).astype(jnp.bfloat16)


def table_kernel(step_ref, vertical_ref, out_ref, made_ref, pairs_ref, table_ref, sems):
    groups = step_ref.shape[1] // ROWS - BUILT

    def departure(g):
        at = pl.ds(g * (ROWS // 2), ROWS // 2)
        return pltpu.make_async_copy(pairs_ref.at[at], out_ref.at[at], sems.at[g])

    def group(g, _):
        here = step_ref.at[:, pl.ds(pl.multiple_of((g + BUILT) * ROWS, ROWS), ROWS)]
        for r in range(ROWS):
            build_table(table_ref.at[r], here, r)
            pairs_ref[g * (ROWS // 2) + r // 2, :, (r % 2) * CHUNK:(r % 2 + 1) * CHUNK] = table_ref[r].T
        departure(g).start()
        return 0

    lax.fori_loop(0, groups, group, 0)
    place_matrices(vertical_ref, *matrices_of(made_ref))
    for g in range(groups):
        departure(g).wait()


def synthesis_kernel(order, points_ref, owners_ref, values_ref, far_table_ref, turns_ref, out_ref,
                     own_ref, table_ref, built_ref, order_ref, coefs_ref, table_sems, sems):
    slots = owners_ref.shape[1]
    tiles = [slice(t, t + 128) for t in range(0, slots, 128)]
    rows, height = own_ref.shape[1:3]

    def arrival(g):
        at = pl.ds(g * (ROWS // 2), ROWS // 2)
        return pltpu.make_async_copy(far_table_ref.at[at], table_ref.at[at], table_sems.at[g])

    def departure(g):
        at = pl.ds(g * ROWS, ROWS)
        return pltpu.make_async_copy(own_ref.at[:, at], out_ref.at[:, at], sems.at[g])

    for g in range(rows // ROWS - BUILT):
        arrival(g).start()
    where = {t: n for n, t in enumerate(order)}
    for slot in range(0, slots, 8):
        parts = []
        for n in range(0, 8, 2):
            pair = values_ref[where[(slot + n) // 2]].astype(jnp.float32)
            parts += [pair[:8], pair[8:]]
        for row, part in enumerate(swap_sublanes(parts)):
            order_ref[slot // 128, row, slot % 128:slot % 128 + 8, :] = part
    for t in range(len(tiles)):
        for row in range(8):
            order_ref[t, row] = order_ref[t, row].T
        for n in range(0, 128, 8):
            parts = swap_sublanes([order_ref[t, row, n:n + 8, :] for row in range(8)])
            for at, part in enumerate(parts):
                coefs_ref[t, n + at] = part

    doubling = jnp.where(owners_ref[...] == 0, 1.0, 2.0)
    sublane = lax.broadcasted_iota(jnp.int32, (8, slots), 0)
    position = lax.broadcasted_iota(jnp.int32, (height, CHUNK), 0) // 4 * CHUNK
    position = position + lax.broadcasted_iota(jnp.int32, (height, CHUNK), 1)

    def group(g, built):
        first = g * ROWS
        if built:
            here = turns_ref.at[:, pl.ds(pl.multiple_of(first, ROWS), ROWS)]
        else:
            arrival(g - BUILT).wait()
        for r in range(ROWS):
            row = first + r
            length = points_ref[row]
            turns = [jnp.broadcast_to(turns_ref[n, pl.ds(row, 1), :], (8, slots)) for n in range(10, 15)]
            chunk, pair, twice = (turns[0], -turns[1]), (turns[2], -turns[3]), turns[4]
            scale = jnp.where(2 * owners_ref[...] < length, doubling, 0.0)
            start = tuple(jnp.where(sublane < 4, 1.0 - c, chunk[c]) * scale for c in range(2))
            values = [
                [coefs_ref[t, c * 64 + row] for t in range(len(tiles))]
                for c in range(2)
            ]
            values = [jnp.concatenate(part, axis=1) for part in values]
            others = [pltpu.roll(part, 4, 0) for part in values]
            turned = []
            for low, high in ((values, others), (others, values)):
                before = multiply(start, [jnp.where(sublane < 4, low[c], high[c]) for c in range(2)])
                value = multiply(before, pair)
                turned += [jnp.concatenate(before, axis=1), jnp.concatenate(value, axis=1)]
                for _ in range(2, height // 8):
                    before, value = value, tuple(twice * value[c] - before[c] for c in range(2))
                    turned.append(jnp.concatenate(value, axis=1))
            turned = jnp.concatenate(turned, axis=0).astype(jnp.bfloat16)
            if built:
                build_table(built_ref.at[r], here, r)
                gridded = times_transposed(turned, built_ref[r])
            else:
                table = table_ref[(g - BUILT) * (ROWS // 2) + r // 2, :, (r % 2) * CHUNK:(r % 2 + 1) * CHUNK]
                gridded = jnp.dot(turned, table, preferred_element_type=jnp.float32)
            for h in range(2):
                own_ref[h, row] = jnp.where(
                    position < length, gridded[h * height:(h + 1) * height], 0.0
                ).astype(jnp.bfloat16)
        departure(g).start()

    for start, end, built in ((0, BUILT, True), (BUILT, rows // ROWS, False)):
        lax.fori_loop(start, end, lambda g, _, built=built: (group(g, built), 0)[1], 0)
    for g in range(rows // ROWS):
        departure(g).wait()


def swap_halves(first, second):
    low = lax.broadcasted_iota(jnp.int32, first.shape, 1) < 64
    return (
        jnp.where(low, first, pltpu.roll(second, 64, 1)),
        jnp.where(low, pltpu.roll(first, 64, 1), second),
    )


def spectral_kernel(order, place_ref, values_ref, legendre_ref, made_ref, out_ref,
                    mixed_ref, back_ref, own_ref, sems):
    levels = made_ref.shape[1] // 4
    copies = {}
    for slot in range(2):
        for q in range(2):
            copies[slot, q] = pltpu.make_async_copy(
                legendre_ref.at[place_ref[0] + slot, q], own_ref.at[slot, q], sems.at[slot, q]
            )
            copies[slot, q].start()
    mix_in, mix_out, parting = (part[...] for part in matrices_of(made_ref))
    where = {t: n for n, t in enumerate(order)}
    for p in range(4):
        bands = [
            jnp.concatenate([values_ref[where[w * 8 + v], :16] for w in range(16)], axis=0)
            for v in (2 * p, 2 * p + 1)
        ]
        mixed = jnp.dot(mix_in, jnp.concatenate(bands, axis=1), preferred_element_type=jnp.float32)
        for c, part in enumerate(swap_halves(mixed[:, :128], mixed[:, 128:])):
            part = part.astype(jnp.bfloat16)
            for k in range(4):
                mixed_ref[k, c * levels:(c + 1) * levels, p * 128:(p + 1) * 128] = (
                    part[k * levels:(k + 1) * levels]
                )
    halves = [
        jnp.concatenate([values_ref[where[w * 8 + v], 16:].astype(jnp.float32) for v in range(8)], axis=0)
        for w in range(16)
    ]
    halves = jnp.concatenate([jnp.concatenate(halves[n:n + 4], axis=1) for n in range(0, 16, 4)], axis=0)
    parted = jnp.dot(halves.astype(jnp.bfloat16), parting, preferred_element_type=jnp.float32)
    parted = [parted[n * levels:(n + 1) * levels] for n in range(4)]
    spreads = [jnp.concatenate([part[:, q * 128:(q + 1) * 128] for part in parted], axis=1) for q in range(2)]
    for slot in range(2):
        parity = place_ref[1 + slot]
        for q in range(2):
            s = (q + parity) % 2
            copies[slot, q].wait()
            values = own_ref[slot, q]
            coefficient = times_transposed(mixed_ref[2 * slot + s], values)
            spread = spreads[q]
            scaled = coefficient * jnp.concatenate([spread, spread], axis=0)
            back_ref[2 * slot + s] = jnp.dot(
                scaled.astype(jnp.bfloat16), values, preferred_element_type=jnp.float32
            )
    for p in range(4):
        lanes = slice(p * 128, (p + 1) * 128)
        halves = [
            jnp.concatenate([back_ref[k, c * levels:(c + 1) * levels, lanes] for k in range(4)], axis=0)
            for c in range(2)
        ]
        parts = jnp.concatenate(swap_halves(*halves), axis=1).astype(jnp.bfloat16)
        remixed = jnp.dot(mix_out, parts, preferred_element_type=jnp.float32).astype(jnp.bfloat16)
        for n in range(2):
            for w in range(16):
                out_ref[where[w * 8 + 2 * p + n]] = remixed[16 * w:16 * w + 16, n * 128:(n + 1) * 128]


def local(grid_field, points, weights, owners, legendre, spectral_variance, vertical):
    _, band_rows, few_levels, longitudes = grid_field.shape
    slots = owners.shape[0]
    levels = vertical.shape[0]
    half_degree, rows = legendre.shape[2:]
    wave, lat = lax.axis_index("wave"), lax.axis_index("lat")
    own = owners.reshape(1, slots)
    parities = lax.dynamic_slice_in_dim(owners, 2 * (wave * lax.axis_size("lat") + lat), 2, 0) % 2
    place = jnp.concatenate([(2 * lat).reshape(1), parities])
    params = pltpu.CompilerParams(vmem_limit_bytes=VMEM_LIMIT)

    order = [int(t) for t in np.random.RandomState(5).permutation(slots // 2)]
    exchange = functools.partial(
        lax.all_to_all, axis_name=("wave", "lat"), split_axis=0, concat_axis=0, axis_index_groups=[order], tiled=True
    )

    chunks = longitudes // CHUNK
    height = chunks * few_levels
    field = grid_field.reshape(2, band_rows, few_levels, chunks, CHUNK).transpose(0, 1, 3, 2, 4)
    field = field.reshape(2, band_rows, height, CHUNK)
    own_spec = pl.BlockSpec((1, slots), lambda g, *_: (0, 0))
    regroup_scratch = [
        pltpu.VMEM((slots // 128, 8, 128, 128), jnp.float32),
        pltpu.VMEM((slots // 128, 8, 128, 128), jnp.float32),
    ]

    far = pl.BlockSpec(memory_space=pltpu.HBM)
    made_shape = (16 * levels, 4 * levels)

    def matrix_spec(shape):
        return pl.BlockSpec(shape, lambda g, *_: (0, 0))

    def blocks_spec(height):
        return pl.BlockSpec((slots // 2, height, 128), lambda g, *_: (0, 0, 0))

    sums, phasors = pl.pallas_call(
        functools.partial(analysis_kernel, order),
        grid_spec=pltpu.PrefetchScalarGridSpec(
            num_scalar_prefetch=3,
            grid=(1,),
            in_specs=[
                own_spec,
                pl.BlockSpec((spectral_variance.shape[0], 128), lambda g, p, w, wave: (0, wave[0] // 2)),
                far,
            ],
            out_specs=[blocks_spec(24), far],
            scratch_shapes=[
                pltpu.VMEM(field.shape, jnp.bfloat16),
                pltpu.VMEM((15, band_rows, slots), jnp.float32),
                pltpu.VMEM((ROWS, CHUNK, 2 * slots), jnp.bfloat16),
                pltpu.VMEM((2, ROWS, 8, slots), jnp.float32),
            ] + regroup_scratch + [
                pltpu.SemaphoreType.DMA((band_rows // ROWS,)),
                pltpu.SemaphoreType.DMA((band_rows // ROWS,)),
            ],
        ),
        out_shape=[
            jax.ShapeDtypeStruct((slots // 2, 24, 128), jnp.bfloat16),
            jax.ShapeDtypeStruct((15, band_rows, slots), jnp.float32),
        ],
        compiler_params=params,
        name="analysis",
    )(points, weights, wave.reshape(1), own, spectral_variance, field)

    arrived = exchange(sums)

    phasors_spec = pl.BlockSpec((15, band_rows, slots), lambda g, *_: (0, 0, 0))
    table_shape = (band_rows // 2 - BUILT * (ROWS // 2), 2 * slots, 2 * CHUNK)
    table, made = pl.pallas_call(
        table_kernel,
        grid=(1,),
        in_specs=[phasors_spec, matrix_spec((levels, levels))],
        out_specs=[far, matrix_spec(made_shape)],
        scratch_shapes=[
            pltpu.VMEM(table_shape, jnp.bfloat16),
            pltpu.VMEM((ROWS, CHUNK, 2 * slots), jnp.bfloat16),
            pltpu.SemaphoreType.DMA((band_rows // ROWS - BUILT,)),
        ],
        out_shape=[
            jax.ShapeDtypeStruct(table_shape, jnp.bfloat16),
            jax.ShapeDtypeStruct(made_shape, jnp.bfloat16),
        ],
        compiler_params=pltpu.CompilerParams(vmem_limit_bytes=50 * 1024 * 1024),
        cost_estimate=pl.CostEstimate(flops=8 * 10**9, bytes_accessed=9 * 10**6, transcendentals=0),
        name="tables",
    )(phasors, vertical)

    remixed = pl.pallas_call(
        functools.partial(spectral_kernel, order),
        grid_spec=pltpu.PrefetchScalarGridSpec(
            num_scalar_prefetch=1,
            grid=(1,),
            in_specs=[blocks_spec(24), far, matrix_spec(made_shape)],
            out_specs=blocks_spec(16),
            scratch_shapes=[
                pltpu.VMEM((4, 2 * levels, rows), jnp.bfloat16),
                pltpu.VMEM((4, 2 * levels, rows), jnp.float32),
                pltpu.VMEM((2, 2, half_degree, rows), jnp.bfloat16),
                pltpu.SemaphoreType.DMA((2, 2)),
            ],
        ),
        out_shape=jax.ShapeDtypeStruct((slots // 2, 16, 128), jnp.bfloat16),
        compiler_params=pltpu.CompilerParams(vmem_limit_bytes=50 * 1024 * 1024),
        name="spectral",
    )(place, arrived, legendre, made)

    returned = exchange(remixed)

    smoothed = pl.pallas_call(
        functools.partial(synthesis_kernel, order),
        grid_spec=pltpu.PrefetchScalarGridSpec(
            num_scalar_prefetch=1,
            grid=(1,),
            in_specs=[own_spec, blocks_spec(16), far, phasors_spec],
            out_specs=far,
            scratch_shapes=[
                pltpu.VMEM(field.shape, jnp.bfloat16),
                pltpu.VMEM(table_shape, jnp.bfloat16),
                pltpu.VMEM((ROWS, CHUNK, 2 * slots), jnp.bfloat16),
                pltpu.VMEM((slots // 128, 8, 128, 128), jnp.float32),
                pltpu.VMEM((slots // 128, 128, 8, 128), jnp.float32),
                pltpu.SemaphoreType.DMA((band_rows // ROWS - BUILT,)),
                pltpu.SemaphoreType.DMA((band_rows // ROWS,)),
            ],
        ),
        out_shape=jax.ShapeDtypeStruct(field.shape, jnp.bfloat16),
        compiler_params=pltpu.CompilerParams(vmem_limit_bytes=50 * 1024 * 1024),
        name="synthesis",
    )(points, own, returned, table, phasors)
    smoothed = smoothed.reshape(2, band_rows, chunks, few_levels, CHUNK).transpose(0, 1, 3, 2, 4)
    return smoothed.reshape(grid_field.shape)


def solution(mesh):
    return jax.shard_map(
        local,
        mesh=mesh,
        in_specs=(
            P(None, "lat", "wave", None),
            P("lat"),
            P("lat"),
            P(),
            P("wave", None, None, None),
            P("lat", None),
            P(),
        ),
        out_specs=P(None, "lat", "wave", None),
        check_vma=False,
    )
```

time: 1270 us -> 65.6 us (0.05)
  other arithmetic: 335 us -> 0.84 us
  loops' own time: 309 us -> 0 us
  local copies, waits for them, and re-layouts: 272 us -> 1.93 us
  waiting for transfers between devices: 244 us -> 10.6 us
  matrix products: 30.4 us -> 0 us
  blocking collectives: 43.4 us -> 17.7 us
  Pallas kernels: 0 us -> 22.6 us
  between operations: 13.7 us -> 0.05 us
    another operation x2 -> x0, loops' own time: 309 us -> none  [the longest x1 295 us: local(): partials = lax.map(partial_sums, jnp.arange(band_rows, dtype=jnp.int32))]
    cos x68 -> x0, other arithmetic: 232 us -> none  [fourier_factors(): factors = jnp.concatenate([jnp.cos(angles), -jnp.sin(angles)], axis=1)]
    reduce_scatter x1 -> x0, waiting for transfers between devices: 194 us -> none  [local(): summed = lax.psum_scatter(partials, 'wave', scatter_dimension=4, tiled=True)]
    dynamic_slice x269 -> x0, local copies, waits for them, and re-layouts: 118 us -> none  [the longest x64 37.7 us: partial_sums(): spectrum = spectrum * (weights[row_index] / row_points.astype(jnp.float32))]
    lt x136 -> x0, other arithmetic: 88.3 us -> none  [the longest x68 44.2 us: fourier_factors(): column_index[:, None] < row_points]
    dynamic_update_slice x68 -> x0, local copies, waits for them, and re-layouts: 52.1 us -> none  [the longest x64 46.7 us: local(): partials = lax.map(partial_sums, jnp.arange(band_rows, dtype=jnp.int32))]
    all_to_all x3 -> x1, waiting for transfers between devices: 49.6 us -> 10.6 us  [local(): arrived = exchange(sums)]
    unnamed x20 -> x10, local copies, waits for them, and re-layouts: 34.4 us -> 1.93 us
  transfers between devices with their start and end apart: 4 -> 1, of which waited for: 4 -> 1; matrix products, arithmetic and copies ran while one was open for 0% -> 1% of each run, Pallas kernels for 0% -> 4%
where the time goes in v1:
time: 65.6 us; the launch traced here: 65.2 us
  Pallas kernels  22.6 us (34%)
  blocking collectives  17.7 us (27%)
  starting transfers between devices  11.5 us (18%)
  waiting for transfers between devices  10.6 us (16%)
  local copies, waits for them, and re-layouts  1.93 us (3%)
  other arithmetic  0.84 us (1%)
    all_to_all x1, blocking collectives, local(): returned = exchange(remixed)  17.7 us
    all_to_all x1, starting transfers between devices, local(): arrived = exchange(sums)  11.5 us
    all_to_all x1, waiting for transfers between devices, local(): arrived = exchange(sums)  10.6 us
    pallas_call x1, Pallas kernels, local(): pl.pallas_call(functools.partial(analysis_kernel, order), grid_spec=pltpu...  9.61 us
    pallas_call x1, Pallas kernels, local(): pl.pallas_call(functools.partial(synthesis_kernel, order), grid_spec=pltp...  6.21 us
    pallas_call x1, Pallas kernels, local(): pl.pallas_call(functools.partial(spectral_kernel, order), grid_spec=pltpu...  3.99 us
    pallas_call x1, Pallas kernels, local(): pl.pallas_call(table_kernel, grid=(1,), in_specs=[phasors_spec, matrix_sp...  2.81 us
    unnamed x10, local copies, waits for them, and re-layouts  1.93 us
  transfers between devices with their start and end apart: 1, of which 1 were waited for; matrix products, arithmetic and copies ran while one was open for 1% of the time, Pallas kernels for 4%

profile of v1, /device:TPU:1, one launch (start us, length us, event | category | flops | bytes accessed | tf_op | source)
XLA Modules:
  0.0 65.2 jit_solution(4776788368995953904)
XLA Ops:
  0.0 9.6 %analysis.1 = (bf16[128,24,128]{2,1,0:T(8,128)(2,1)}, f32[15,64,256]{2,1,0:T(8,128)}) custom-call(s32[64]{0:T(128)} %points_ref.3, f32[64]{0:T(128)} %weights_ref.1, s32[1]{0:T(128)} %bitcast.2.wave_ref, s32[1,256]{1,0:T(1,128)} %bitcast.13, f32[8,1024]{1,0:T(8,128)} %variance_ref.1, bf16[2,64,64,128]{3,2,1,0:T(8,128)(2,1)} %bitcast.15), custom_call_target="tpu_custom_call" | custom-call | tf_op jit(solution)/shard_map/analysis/pallas_call | solution.py:430
  9.6 11.5 %all-to-all-start = ((bf16[128,24,128]{2,1,0:T(8,128)(2,1)}), bf16[128,24,128]{2,1,0:T(8,128)(2,1)S(1)}, u32[]{:S(2)}, u32[]{:S(2)}) async-start(bf16[128,24,128]{2,1,0:T(8,128)(2,1)} %get-tuple-element.9), calls=%async_computation | async-start | bytes 1572864 | tf_op jit(solution)/shard_map/all_to_all | solution.py:459
  21.1 0.8 %and_select_fusion = s32[2]{0:T(128)S(1)} fusion(s32[256]{0:T(256)} %param.10, s32[]{:T(128)S(6)} %select_n.10), kind=kLoop, calls=%fused_computation.2 | loop fusion | flops 22 | bytes 20 | tf_op jit(solution)/shard_map/jit(remainder)/select_n | solution.py:402
  21.9 0.1 pad_add_fusion.place_ref
  22.0 0.0 copy-start
  22.0 1.2 %copy-done = f32[15,64,256]{2,1,0:T(8,128)S(1)} copy-done((f32[15,64,256]{2,1,0:T(8,128)S(1)}, f32[15,64,256]{2,1,0:T(8,128)}, u32[]{:S(2)}) %copy-start) | copy-done | bytes 983064
  23.2 0.0 copy-start.4
  23.2 0.7 %copy-done.4 = bf16[64,64]{1,0:T(8,128)(2,1)S(1)} copy-done((bf16[64,64]{1,0:T(8,128)(2,1)S(1)}, bf16[64,64]{1,0:T(8,128)(2,1)}, u32[]{:S(2)}) %copy-start.4) | copy-done | bytes 8216
  23.9 2.8 %tables.1 = (bf16[20,512,256]{2,1,0:T(8,128)(2,1)}, bf16[1024,256]{1,0:T(8,128)(2,1)S(1)}) custom-call(f32[15,64,256]{2,1,0:T(8,128)S(1)} %copy-done, bf16[64,64]{1,0:T(8,128)(2,1)S(1)} %copy-done.4), custom_call_target="tpu_custom_call" | custom-call | flops 8000000000 | bytes 9000000 | tf_op jit(solution)/shard_map/tables/pallas_call | solution.py:463
  26.7 10.6 %all-to-all-done.values_ref = bf16[128,24,128]{2,1,0:T(8,128)(2,1)S(1)} async-done(((bf16[128,24,128]{2,1,0:T(8,128)(2,1)}), bf16[128,24,128]{2,1,0:T(8,128)(2,1)S(1)}, u32[]{:S(2)}, u32[]{:S(2)}) %all-to-all-start) | async-done | bytes 786464 | tf_op jit(solution)/shard_map/all_to_all | solution.py:459
  37.3 0.0 copy-start.1
  37.3 0.0 copy-start.2
  37.3 0.0 copy-start.3
  37.3 4.0 %spectral.1 = bf16[128,16,128]{2,1,0:T(8,128)(2,1)S(1)} custom-call(s32[3]{0:T(128)S(1)} %pad_add_fusion.place_ref, bf16[128,24,128]{2,1,0:T(8,128)(2,1)S(1)} %all-to-all-done.values_ref, bf16[16,2,512,512]{3,2,1,0:T(8,128)(2,1)} %legendre_ref.1, bf16[1024,256]{1,0:T(8,128)(2,1)S(1)} %get-tuple-element.11.made_ref), custom_call_target="tpu_custom_call" | custom-call | tf_op jit(solution)/shard_map/spectral/pallas_call | solution.py:482
  41.3 17.7 %all_to_all.10.values_ref = bf16[128,16,128]{2,1,0:T(8,128)(2,1)S(1)} all-to-all(bf16[128,16,128]{2,1,0:T(8,128)(2,1)S(1)} %spectral.1), channel_id=1, replica_groups={{58,38,18,114,13,119,33,109,9,44,22,67,116,77,121,8,101,6,104,96,93,75,..., dimensions={0} | all-to-all | bytes 1048576 | tf_op jit(solution)/shard_map/all_to_all | solution.py:501
  59.0 0.0 copy-done.1
  59.0 0.0 copy-done.2
  59.0 0.0 copy-done.3
  59.0 6.2 %synthesis.1 = bf16[2,64,64,128]{3,2,1,0:T(8,128)(2,1)} custom-call(s32[64]{0:T(128)S(1)} %copy-done.3, s32[1,256]{1,0:T(1,128)S(1)} %bitcast.14, bf16[128,16,128]{2,1,0:T(8,128)(2,1)S(1)} %all_to_all.10.values_ref, bf16[20,512,256]{2,1,0:T(8,128)(2,1)} %get-tuple-element.12.far_table_ref, f32[15,64,256]{2,1,0:T(8,128)S(1)} %copy-done.1), custom_call_target="tpu_custom_call" | custom-call | tf_op jit(solution)/shard_map/synthesis/pallas_call | solution.py:503
Async XLA Ops:
  9.6 27.7 %all-to-all-start = ((bf16[128,24,128]{2,1,0:T(8,128)(2,1)}), bf16[128,24,128]{2,1,0:T(8,128)(2,1)S(1)}, u32[]{:S(2)}, u32[]{:S(2)}) async-start(bf16[128,24,128]{2,1,0:T(8,128)(2,1)} %get-tuple-element.9), calls=%async_computation | async-start | bytes 1572864 | tf_op jit(solution)/shard_map/all_to_all | solution.py:459
  22.0 1.2 %copy-start = (f32[15,64,256]{2,1,0:T(8,128)S(1)}, f32[15,64,256]{2,1,0:T(8,128)}, u32[]{:S(2)}) copy-start(f32[15,64,256]{2,1,0:T(8,128)} %get-tuple-element.10.step_ref.turns_ref) | copy-start | bytes 2949124
  23.2 0.7 %copy-start.4 = (bf16[64,64]{1,0:T(8,128)(2,1)S(1)}, bf16[64,64]{1,0:T(8,128)(2,1)}, u32[]{:S(2)}) copy-start(bf16[64,64]{1,0:T(8,128)(2,1)} %vertical_ref.1) | copy-start | bytes 24580
  37.3 21.7 %copy-start.1 = (f32[15,64,256]{2,1,0:T(8,128)S(1)}, f32[15,64,256]{2,1,0:T(8,128)}, u32[]{:S(2)}) copy-start(f32[15,64,256]{2,1,0:T(8,128)} %get-tuple-element.10.step_ref.turns_ref) | copy-start | bytes 2949124
  37.3 21.7 %copy-start.2 = (s32[256]{0:T(256)S(1)}, s32[256]{0:T(256)}, u32[]{:S(2)}) copy-start(s32[256]{0:T(256)} %param.10) | copy-start | bytes 3076
  37.3 21.7 %copy-start.3 = (s32[64]{0:T(128)S(1)}, s32[64]{0:T(128)}, u32[]{:S(2)}) copy-start(s32[64]{0:T(128)} %points_ref.3) | copy-start | bytes 772

commit v2 on v1

--- a/solution.py
+++ b/solution.py
@@ -10,7 +10,8 @@
 
 ROWS = 8
 CHUNK = 128
-BUILT = 3
+APART = 1024
+BUILT = 2
 VMEM_LIMIT = 56 * 1024 * 1024
 
 SIN_TERMS = (3.141592640130707, -5.167710083507862, 2.550077523214134, -0.5982912856178576, 0.0776576603009221)
@@ -57,13 +58,13 @@
 def place_phasors(step_ref, waves, lengths, inverse):
     cosine, sine = phasor(waves, lengths, inverse)
     turn, at = (cosine, -sine), 1
-    keep = {1: 0, 2: 2, 4: 4, 8: 6, CHUNK: 10, 2 * CHUNK: 12}
+    keep = {1: 0, 2: 2, 4: 4, 8: 6, CHUNK: 10, 2 * CHUNK: 12, APART: 15}
     while True:
         if at in keep:
             step_ref[keep[at]], step_ref[keep[at] + 1] = turn
         if at in (8, 16, 2 * CHUNK):
             step_ref[{8: 8, 16: 9, 2 * CHUNK: 14}[at]] = 2.0 * turn[0]
-        if at == 2 * CHUNK:
+        if at == APART:
             break
         turn, at = square(turn), 2 * at
 
@@ -97,19 +98,18 @@
     real, imaginary, twice, twice_next = steps_of(step_ref, (6, 7, 8, 9), r)
     values = [multiply(multiply(powers[0], powers[1]), powers[2])]
     values.append(multiply(values[0], (real, imaginary)))
-    for n in range(2, size // 8):
-        if n < 4:
-            values.append(tuple(twice * values[n - 1][c] - values[n - 2][c] for c in range(2)))
-        else:
-            values.append(tuple(twice_next * values[n - 2][c] - values[n - 4][c] for c in range(2)))
-        if n % 2:
-            for c in range(2):
-                both = jnp.concatenate([values[n - 1][c], values[n][c]], axis=0).astype(jnp.bfloat16)
-                table_ref[8 * n - 8:8 * n + 8, c * slots:(c + 1) * slots] = both
-        elif n == 2:
-            for c in range(2):
-                both = jnp.concatenate([values[0][c], values[1][c]], axis=0).astype(jnp.bfloat16)
-                table_ref[:16, c * slots:(c + 1) * slots] = both
+    for top in range(0, table_ref.shape[0], CHUNK):
+        if top:
+            values = [multiply(value, steps_of(step_ref, (15, 16), r)) for value in values[:2]]
+        for n in range(2, CHUNK // 8 + 2):
+            if n % 2 == 0:
+                for c in range(2):
+                    both = jnp.concatenate([values[n - 2][c], values[n - 1][c]], axis=0).astype(jnp.bfloat16)
+                    table_ref[top + 8 * n - 16:top + 8 * n, c * slots:(c + 1) * slots] = both
+            if n < 4:
+                values.append(tuple(twice * values[n - 1][c] - values[n - 2][c] for c in range(2)))
+            elif n < CHUNK // 8:
+                values.append(tuple(twice_next * values[n - 2][c] - values[n - 4][c] for c in range(2)))
 
 
 def analysis_kernel(order, points_ref, weights_ref, wave_ref, owners_ref, variance_ref, field_ref, out_ref,
@@ -124,7 +124,7 @@
 
     def departure(g):
         at = pl.ds(pl.multiple_of(g * ROWS, ROWS), ROWS)
-        return pltpu.make_async_copy(step_ref.at[:, at], phasors_ref.at[:, at], phasor_sems.at[g])
+        return pltpu.make_async_copy(step_ref.at[:15, at], phasors_ref.at[:, at], phasor_sems.at[g])
 
     for g in range(rows // ROWS):
         arrival(g).start()
@@ -132,6 +132,8 @@
     sublane = lax.broadcasted_iota(jnp.int32, (8, slots), 0)
     position = lax.broadcasted_iota(jnp.int32, (height, CHUNK), 0) // 4 * CHUNK
     position = position + lax.broadcasted_iota(jnp.int32, (height, CHUNK), 1)
+    half = height // 2
+    position = jnp.concatenate([position[:half], position[half:]], axis=1)
 
     def group(g, _):
         first = g * ROWS
@@ -145,14 +147,18 @@
 
             build_table(table_ref.at[r], here, r)
             inside = jnp.where(position < length, 1.0, 0.0).astype(jnp.bfloat16)
-            points = jnp.concatenate([own_ref[0, first + r] * inside, own_ref[1, first + r] * inside], axis=0)
+            points = [
+                jnp.concatenate([own_ref[n, first + r, :half, :], own_ref[n, first + r, half:, :]], axis=1) * inside
+                for n in range(2)
+            ]
+            points = jnp.concatenate(points, axis=0)
             parts = jnp.dot(points, table_ref[r], preferred_element_type=jnp.float32)
             chunk, pair, twice = steps_of(here, (10, 11), r), steps_of(here, (12, 13), r), steps_of(here, (14,), r)[0]
             sums = []
             for h in range(2):
                 blocks = [
                     tuple(parts[b:b + 8, c * slots:(c + 1) * slots] for c in range(2))
-                    for b in range(h * height, (h + 1) * height, 8)
+                    for b in range(h * half, (h + 1) * half, 8)
                 ]
                 later, total = blocks[-1], tuple(blocks[-2][c] + twice * blocks[-1][c] for c in range(2))
                 for part in blocks[-3:0:-1]:
@@ -440,8 +446,8 @@
             out_specs=[blocks_spec(24), far],
             scratch_shapes=[
                 pltpu.VMEM(field.shape, jnp.bfloat16),
-                pltpu.VMEM((15, band_rows, slots), jnp.float32),
-                pltpu.VMEM((ROWS, CHUNK, 2 * slots), jnp.bfloat16),
+                pltpu.VMEM((17, band_rows, slots), jnp.float32),
+                pltpu.VMEM((ROWS, 2 * CHUNK, 2 * slots), jnp.bfloat16),
                 pltpu.VMEM((2, ROWS, 8, slots), jnp.float32),
             ] + regroup_scratch + [
                 pltpu.SemaphoreType.DMA((band_rows // ROWS,)),

time: 65.6 us -> 65.8 us (level)
  transfers between devices with their start and end apart: 1 -> 1, of which waited for: 1 -> 1; matrix products, arithmetic and copies ran while one was open for 1% -> 1% of each run, Pallas kernels for 4% -> 5%
where the time goes in v2:
time: 65.8 us; the launch traced here: 65.5 us
  Pallas kernels  23.2 us (35%)
  blocking collectives  17.7 us (27%)
  starting transfers between devices  11.5 us (17%)
  waiting for transfers between devices  10.2 us (16%)
  local copies, waits for them, and re-layouts  1.93 us (3%)
  other arithmetic  0.84 us (1%)
    all_to_all x1, blocking collectives, local(): returned = exchange(remixed)  17.7 us
    all_to_all x1, starting transfers between devices, local(): arrived = exchange(sums)  11.5 us
    all_to_all x1, waiting for transfers between devices, local(): arrived = exchange(sums)  10.2 us
    pallas_call x1, Pallas kernels, local(): pl.pallas_call(functools.partial(analysis_kernel, order), grid_spec=pltpu...  10 us
    pallas_call x1, Pallas kernels, local(): pl.pallas_call(functools.partial(synthesis_kernel, order), grid_spec=pltp...  6.03 us
    pallas_call x1, Pallas kernels, local(): pl.pallas_call(functools.partial(spectral_kernel, order), grid_spec=pltpu...  3.98 us
    pallas_call x1, Pallas kernels, local(): pl.pallas_call(table_kernel, grid=(1,), in_specs=[phasors_spec, matrix_sp...  3.19 us
    unnamed x10, local copies, waits for them, and re-layouts  1.93 us
  transfers between devices with their start and end apart: 1, of which 1 were waited for; matrix products, arithmetic and copies ran while one was open for 1% of the time, Pallas kernels for 5%

profile of v2, /device:TPU:1, one launch (start us, length us, event | category | flops | bytes accessed | tf_op | source)
XLA Modules:
  0.0 65.5 jit_solution(1262510069556870221)
XLA Ops:
  0.0 10.0 %analysis.1 = (bf16[128,24,128]{2,1,0:T(8,128)(2,1)}, f32[15,64,256]{2,1,0:T(8,128)}) custom-call(s32[64]{0:T(128)} %points_ref.3, f32[64]{0:T(128)} %weights_ref.1, s32[1]{0:T(128)} %bitcast.2.wave_ref, s32[1,256]{1,0:T(1,128)} %bitcast.13, f32[8,1024]{1,0:T(8,128)} %variance_ref.1, bf16[2,64,64,128]{3,2,1,0:T(8,128)(2,1)} %bitcast.15), custom_call_target="tpu_custom_call" | custom-call | tf_op jit(solution)/shard_map/analysis/pallas_call | solution.py:436
  10.0 11.5 %all-to-all-start = ((bf16[128,24,128]{2,1,0:T(8,128)(2,1)}), bf16[128,24,128]{2,1,0:T(8,128)(2,1)S(1)}, u32[]{:S(2)}, u32[]{:S(2)}) async-start(bf16[128,24,128]{2,1,0:T(8,128)(2,1)} %get-tuple-element.9), calls=%async_computation | async-start | bytes 1572864 | tf_op jit(solution)/shard_map/all_to_all | solution.py:465
  21.6 0.8 %and_select_fusion = s32[2]{0:T(128)S(1)} fusion(s32[256]{0:T(256)} %param.10, s32[]{:T(128)S(6)} %select_n.10), kind=kLoop, calls=%fused_computation.2 | loop fusion | flops 22 | bytes 20 | tf_op jit(solution)/shard_map/jit(remainder)/select_n | solution.py:408
  22.3 0.1 pad_add_fusion.place_ref
  22.4 0.0 copy-start
  22.4 1.2 %copy-done = f32[15,64,256]{2,1,0:T(8,128)S(1)} copy-done((f32[15,64,256]{2,1,0:T(8,128)S(1)}, f32[15,64,256]{2,1,0:T(8,128)}, u32[]{:S(2)}) %copy-start) | copy-done | bytes 983064
  23.6 0.0 copy-start.4
  23.6 0.7 %copy-done.4 = bf16[64,64]{1,0:T(8,128)(2,1)S(1)} copy-done((bf16[64,64]{1,0:T(8,128)(2,1)S(1)}, bf16[64,64]{1,0:T(8,128)(2,1)}, u32[]{:S(2)}) %copy-start.4) | copy-done | bytes 8216
  24.3 3.2 %tables.1 = (bf16[24,512,256]{2,1,0:T(8,128)(2,1)}, bf16[1024,256]{1,0:T(8,128)(2,1)S(1)}) custom-call(f32[15,64,256]{2,1,0:T(8,128)S(1)} %copy-done, bf16[64,64]{1,0:T(8,128)(2,1)S(1)} %copy-done.4), custom_call_target="tpu_custom_call" | custom-call | flops 8000000000 | bytes 9000000 | tf_op jit(solution)/shard_map/tables/pallas_call | solution.py:469
  27.5 10.2 %all-to-all-done.values_ref = bf16[128,24,128]{2,1,0:T(8,128)(2,1)S(1)} async-done(((bf16[128,24,128]{2,1,0:T(8,128)(2,1)}), bf16[128,24,128]{2,1,0:T(8,128)(2,1)S(1)}, u32[]{:S(2)}, u32[]{:S(2)}) %all-to-all-start) | async-done | bytes 786464 | tf_op jit(solution)/shard_map/all_to_all | solution.py:465
  37.7 0.0 copy-start.1
  37.7 0.0 copy-start.2
  37.7 0.0 copy-start.3
  37.7 4.0 %spectral.1 = bf16[128,16,128]{2,1,0:T(8,128)(2,1)S(1)} custom-call(s32[3]{0:T(128)S(1)} %pad_add_fusion.place_ref, bf16[128,24,128]{2,1,0:T(8,128)(2,1)S(1)} %all-to-all-done.values_ref, bf16[16,2,512,512]{3,2,1,0:T(8,128)(2,1)} %legendre_ref.1, bf16[1024,256]{1,0:T(8,128)(2,1)S(1)} %get-tuple-element.11.made_ref), custom_call_target="tpu_custom_call" | custom-call | tf_op jit(solution)/shard_map/spectral/pallas_call | solution.py:488
  41.7 17.7 %all_to_all.10.values_ref = bf16[128,16,128]{2,1,0:T(8,128)(2,1)S(1)} all-to-all(bf16[128,16,128]{2,1,0:T(8,128)(2,1)S(1)} %spectral.1), channel_id=1, replica_groups={{58,38,18,114,13,119,33,109,9,44,22,67,116,77,121,8,101,6,104,96,93,75,..., dimensions={0} | all-to-all | bytes 1048576 | tf_op jit(solution)/shard_map/all_to_all | solution.py:507
  59.4 0.0 copy-done.1
  59.4 0.0 copy-done.2
  59.4 0.0 copy-done.3
  59.4 6.0 %synthesis.1 = bf16[2,64,64,128]{3,2,1,0:T(8,128)(2,1)} custom-call(s32[64]{0:T(128)S(1)} %copy-done.3, s32[1,256]{1,0:T(1,128)S(1)} %bitcast.14, bf16[128,16,128]{2,1,0:T(8,128)(2,1)S(1)} %all_to_all.10.values_ref, bf16[24,512,256]{2,1,0:T(8,128)(2,1)} %get-tuple-element.12.far_table_ref, f32[15,64,256]{2,1,0:T(8,128)S(1)} %copy-done.1), custom_call_target="tpu_custom_call" | custom-call | tf_op jit(solution)/shard_map/synthesis/pallas_call | solution.py:509
Async XLA Ops:
  10.0 27.7 %all-to-all-start = ((bf16[128,24,128]{2,1,0:T(8,128)(2,1)}), bf16[128,24,128]{2,1,0:T(8,128)(2,1)S(1)}, u32[]{:S(2)}, u32[]{:S(2)}) async-start(bf16[128,24,128]{2,1,0:T(8,128)(2,1)} %get-tuple-element.9), calls=%async_computation | async-start | bytes 1572864 | tf_op jit(solution)/shard_map/all_to_all | solution.py:465
  22.4 1.2 %copy-start = (f32[15,64,256]{2,1,0:T(8,128)S(1)}, f32[15,64,256]{2,1,0:T(8,128)}, u32[]{:S(2)}) copy-start(f32[15,64,256]{2,1,0:T(8,128)} %get-tuple-element.10.step_ref.turns_ref) | copy-start | bytes 2949124
  23.6 0.7 %copy-start.4 = (bf16[64,64]{1,0:T(8,128)(2,1)S(1)}, bf16[64,64]{1,0:T(8,128)(2,1)}, u32[]{:S(2)}) copy-start(bf16[64,64]{1,0:T(8,128)(2,1)} %vertical_ref.1) | copy-start | bytes 24580
  37.7 21.7 %copy-start.1 = (f32[15,64,256]{2,1,0:T(8,128)S(1)}, f32[15,64,256]{2,1,0:T(8,128)}, u32[]{:S(2)}) copy-start(f32[15,64,256]{2,1,0:T(8,128)} %get-tuple-element.10.step_ref.turns_ref) | copy-start | bytes 2949124
  37.7 21.7 %copy-start.2 = (s32[256]{0:T(256)S(1)}, s32[256]{0:T(256)}, u32[]{:S(2)}) copy-start(s32[256]{0:T(256)} %param.10) | copy-start | bytes 3076
  37.7 21.7 %copy-start.3 = (s32[64]{0:T(128)S(1)}, s32[64]{0:T(128)}, u32[]{:S(2)}) copy-start(s32[64]{0:T(128)} %points_ref.3) | copy-start | bytes 772

commit v3 on v1

--- a/solution.py
+++ b/solution.py
@@ -10,7 +10,7 @@
 
 ROWS = 8
 CHUNK = 128
-BUILT = 3
+BUILT = 2
 VMEM_LIMIT = 56 * 1024 * 1024
 
 SIN_TERMS = (3.141592640130707, -5.167710083507862, 2.550077523214134, -0.5982912856178576, 0.0776576603009221)
@@ -133,17 +133,21 @@
     position = lax.broadcasted_iota(jnp.int32, (height, CHUNK), 0) // 4 * CHUNK
     position = position + lax.broadcasted_iota(jnp.int32, (height, CHUNK), 1)
 
-    def group(g, _):
+    def group(g, early):
         first = g * ROWS
         lengths, inverse = lengths_by_row(points_ref, first, (ROWS, slots))
         here = step_ref.at[:, pl.ds(pl.multiple_of(first, ROWS), ROWS)]
         place_phasors(here, waves, lengths, inverse)
         departure(g).start()
+        if early:
+            for r in range(ROWS):
+                build_table(table_ref.at[r], here, r)
         arrival(g).wait()
         for r in range(ROWS):
             length = points_ref[first + r]
 
-            build_table(table_ref.at[r], here, r)
+            if not early:
+                build_table(table_ref.at[r], here, r)
             inside = jnp.where(position < length, 1.0, 0.0).astype(jnp.bfloat16)
             points = jnp.concatenate([own_ref[0, first + r] * inside, own_ref[1, first + r] * inside], axis=0)
             parts = jnp.dot(points, table_ref[r], preferred_element_type=jnp.float32)
@@ -173,9 +177,9 @@
             for t, lanes in enumerate(tiles):
                 for row, part in enumerate(swap_sublanes([rows_ref[c, r, :, lanes] for r in range(ROWS)])):
                     sums_ref[t, row, pl.ds(pl.multiple_of(c * 64 + first, 8), 8), :] = part
-        return 0
-
-    lax.fori_loop(0, rows // ROWS, group, 0)
+
+    group(0, True)
+    lax.fori_loop(1, rows // ROWS, lambda g, _: (group(g, False), 0)[1], 0)
 
     for row in range(8):
         for t in range(len(tiles)):
@@ -244,8 +248,9 @@
         departure(g).wait()
 
 
-def synthesis_kernel(order, points_ref, owners_ref, values_ref, far_table_ref, turns_ref, out_ref,
-                     own_ref, table_ref, built_ref, order_ref, coefs_ref, table_sems, sems):
+def synthesis_kernel(order, points_ref, owners_ref, near_values_ref, far_table_ref, near_turns_ref, out_ref,
+                     values_ref, turns_ref, own_ref, table_ref, built_ref, order_ref, coefs_ref,
+                     near_sems, table_sems, sems):
     slots = owners_ref.shape[1]
     tiles = [slice(t, t + 128) for t in range(0, slots, 128)]
     rows, height = own_ref.shape[1:3]
@@ -258,8 +263,15 @@
         at = pl.ds(g * ROWS, ROWS)
         return pltpu.make_async_copy(own_ref.at[:, at], out_ref.at[:, at], sems.at[g])
 
+    near = [
+        pltpu.make_async_copy(near_values_ref, values_ref, near_sems.at[0]),
+        pltpu.make_async_copy(near_turns_ref, turns_ref, near_sems.at[1]),
+    ]
+    for copy in near:
+        copy.start()
     for g in range(rows // ROWS - BUILT):
         arrival(g).start()
+    near[0].wait()
     where = {t: n for n, t in enumerate(order)}
     for slot in range(0, slots, 8):
         parts = []
@@ -321,6 +333,7 @@
                 ).astype(jnp.bfloat16)
         departure(g).start()
 
+    near[1].wait()
     for start, end, built in ((0, BUILT, True), (BUILT, rows // ROWS, False)):
         lax.fori_loop(start, end, lambda g, _, built=built: (group(g, built), 0)[1], 0)
     for g in range(rows // ROWS):
@@ -335,9 +348,13 @@
     )
 
 
-def spectral_kernel(order, place_ref, values_ref, legendre_ref, made_ref, out_ref,
-                    mixed_ref, back_ref, own_ref, sems):
+def spectral_kernel(order, place_ref, near_values_ref, legendre_ref, near_made_ref, out_ref,
+                    values_ref, made_ref, mixed_ref, back_ref, own_ref, near_sems, sems):
     levels = made_ref.shape[1] // 4
+    near = [
+        pltpu.make_async_copy(near_made_ref, made_ref, near_sems.at[0]),
+        pltpu.make_async_copy(near_values_ref, values_ref, near_sems.at[1]),
+    ]
     copies = {}
     for slot in range(2):
         for q in range(2):
@@ -345,6 +362,10 @@
                 legendre_ref.at[place_ref[0] + slot, q], own_ref.at[slot, q], sems.at[slot, q]
             )
             copies[slot, q].start()
+    for copy in near:
+        copy.start()
+    for copy in near:
+        copy.wait()
     mix_in, mix_out, parting = (part[...] for part in matrices_of(made_ref))
     where = {t: n for n, t in enumerate(order)}
     for p in range(4):
@@ -419,6 +440,7 @@
     ]
 
     far = pl.BlockSpec(memory_space=pltpu.HBM)
+    anywhere = pl.BlockSpec(memory_space=pl.ANY)
     made_shape = (16 * levels, 4 * levels)
 
     def matrix_spec(shape):
@@ -484,12 +506,15 @@
         grid_spec=pltpu.PrefetchScalarGridSpec(
             num_scalar_prefetch=1,
             grid=(1,),
-            in_specs=[blocks_spec(24), far, matrix_spec(made_shape)],
+            in_specs=[anywhere, far, anywhere],
             out_specs=blocks_spec(16),
             scratch_shapes=[
+                pltpu.VMEM((slots // 2, 24, 128), jnp.bfloat16),
+                pltpu.VMEM(made_shape, jnp.bfloat16),
                 pltpu.VMEM((4, 2 * levels, rows), jnp.bfloat16),
                 pltpu.VMEM((4, 2 * levels, rows), jnp.float32),
                 pltpu.VMEM((2, 2, half_degree, rows), jnp.bfloat16),
+                pltpu.SemaphoreType.DMA((2,)),
                 pltpu.SemaphoreType.DMA((2, 2)),
             ],
         ),
@@ -505,14 +530,17 @@
         grid_spec=pltpu.PrefetchScalarGridSpec(
             num_scalar_prefetch=1,
             grid=(1,),
-            in_specs=[own_spec, blocks_spec(16), far, phasors_spec],
+            in_specs=[own_spec, anywhere, far, anywhere],
             out_specs=far,
             scratch_shapes=[
+                pltpu.VMEM((slots // 2, 16, 128), jnp.bfloat16),
+                pltpu.VMEM((15, band_rows, slots), jnp.float32),
                 pltpu.VMEM(field.shape, jnp.bfloat16),
                 pltpu.VMEM(table_shape, jnp.bfloat16),
                 pltpu.VMEM((ROWS, CHUNK, 2 * slots), jnp.bfloat16),
                 pltpu.VMEM((slots // 128, 8, 128, 128), jnp.float32),
                 pltpu.VMEM((slots // 128, 128, 8, 128), jnp.float32),
+                pltpu.SemaphoreType.DMA((2,)),
                 pltpu.SemaphoreType.DMA((band_rows // ROWS - BUILT,)),
                 pltpu.SemaphoreType.DMA((band_rows // ROWS,)),
             ],

time: 65.6 us -> 65.7 us (level)
  transfers between devices with their start and end apart: 1 -> 1, of which waited for: 1 -> 1; matrix products, arithmetic and copies ran while one was open for 1% -> 1% of each run, Pallas kernels for 4% -> 5%
where the time goes in v3:
time: 65.7 us; the launch traced here: 65.4 us
  Pallas kernels  23.2 us (35%)
  blocking collectives  17.7 us (27%)
  starting transfers between devices  11.5 us (18%)
  waiting for transfers between devices  10.2 us (16%)
  local copies, waits for them, and re-layouts  1.93 us (3%)
  other arithmetic  0.84 us (1%)
    all_to_all x1, blocking collectives, local(): returned = exchange(remixed)  17.7 us
    all_to_all x1, starting transfers between devices, local(): arrived = exchange(sums)  11.5 us
    all_to_all x1, waiting for transfers between devices, local(): arrived = exchange(sums)  10.2 us
    pallas_call x1, Pallas kernels, local(): pl.pallas_call(functools.partial(analysis_kernel, order), grid_spec=pltpu...  9.63 us
    pallas_call x1, Pallas kernels, local(): pl.pallas_call(functools.partial(synthesis_kernel, order), grid_spec=pltp...  6.35 us
    pallas_call x1, Pallas kernels, local(): pl.pallas_call(functools.partial(spectral_kernel, order), grid_spec=pltpu...  4 us
    pallas_call x1, Pallas kernels, local(): pl.pallas_call(table_kernel, grid=(1,), in_specs=[phasors_spec, matrix_sp...  3.19 us
    unnamed x10, local copies, waits for them, and re-layouts  1.93 us
  transfers between devices with their start and end apart: 1, of which 1 were waited for; matrix products, arithmetic and copies ran while one was open for 1% of the time, Pallas kernels for 5%

profile of v3, /device:TPU:1, one launch (start us, length us, event | category | flops | bytes accessed | tf_op | source)
XLA Modules:
  0.0 65.4 jit_solution(12162887767540115976)
XLA Ops:
  0.0 9.6 %analysis.1 = (bf16[128,24,128]{2,1,0:T(8,128)(2,1)}, f32[15,64,256]{2,1,0:T(8,128)}) custom-call(s32[64]{0:T(128)} %points_ref.3, f32[64]{0:T(128)} %weights_ref.1, s32[1]{0:T(128)} %bitcast.2.wave_ref, s32[1,256]{1,0:T(1,128)} %bitcast.13, f32[8,1024]{1,0:T(8,128)} %variance_ref.1, bf16[2,64,64,128]{3,2,1,0:T(8,128)(2,1)} %bitcast.15), custom_call_target="tpu_custom_call" | custom-call | tf_op jit(solution)/shard_map/analysis/pallas_call | solution.py:452
  9.6 11.5 %all-to-all-start = ((bf16[128,24,128]{2,1,0:T(8,128)(2,1)}), bf16[128,24,128]{2,1,0:T(8,128)(2,1)S(1)}, u32[]{:S(2)}, u32[]{:S(2)}) async-start(bf16[128,24,128]{2,1,0:T(8,128)(2,1)} %get-tuple-element.9), calls=%async_computation | async-start | bytes 1572864 | tf_op jit(solution)/shard_map/all_to_all | solution.py:481
  21.1 0.8 %and_select_fusion = s32[2]{0:T(128)S(1)} fusion(s32[256]{0:T(256)} %param.10, s32[]{:T(128)S(6)} %select_n.10), kind=kLoop, calls=%fused_computation.2 | loop fusion | flops 22 | bytes 20 | tf_op jit(solution)/shard_map/jit(remainder)/select_n | solution.py:423
  21.9 0.1 pad_add_fusion.place_ref
  22.0 0.0 copy-start
  22.0 1.2 %copy-done = f32[15,64,256]{2,1,0:T(8,128)S(1)} copy-done((f32[15,64,256]{2,1,0:T(8,128)S(1)}, f32[15,64,256]{2,1,0:T(8,128)}, u32[]{:S(2)}) %copy-start) | copy-done | bytes 983064
  23.2 0.0 copy-start.4
  23.2 0.7 %copy-done.4 = bf16[64,64]{1,0:T(8,128)(2,1)S(1)} copy-done((bf16[64,64]{1,0:T(8,128)(2,1)S(1)}, bf16[64,64]{1,0:T(8,128)(2,1)}, u32[]{:S(2)}) %copy-start.4) | copy-done | bytes 8216
  23.9 3.2 %tables.1 = (bf16[24,512,256]{2,1,0:T(8,128)(2,1)}, bf16[1024,256]{1,0:T(8,128)(2,1)S(1)}) custom-call(f32[15,64,256]{2,1,0:T(8,128)S(1)} %copy-done, bf16[64,64]{1,0:T(8,128)(2,1)S(1)} %copy-done.4), custom_call_target="tpu_custom_call" | custom-call | flops 8000000000 | bytes 9000000 | tf_op jit(solution)/shard_map/tables/pallas_call | solution.py:485
  27.1 10.2 %all-to-all-done.near_values_ref = bf16[128,24,128]{2,1,0:T(8,128)(2,1)S(1)} async-done(((bf16[128,24,128]{2,1,0:T(8,128)(2,1)}), bf16[128,24,128]{2,1,0:T(8,128)(2,1)S(1)}, u32[]{:S(2)}, u32[]{:S(2)}) %all-to-all-start) | async-done | bytes 786464 | tf_op jit(solution)/shard_map/all_to_all | solution.py:481
  37.3 0.0 copy-start.1
  37.3 0.0 copy-start.2
  37.3 0.0 copy-start.3
  37.3 4.0 %spectral.1 = bf16[128,16,128]{2,1,0:T(8,128)(2,1)S(1)} custom-call(s32[3]{0:T(128)S(1)} %pad_add_fusion.place_ref, bf16[128,24,128]{2,1,0:T(8,128)(2,1)S(1)} %all-to-all-done.near_values_ref, bf16[16,2,512,512]{3,2,1,0:T(8,128)(2,1)} %legendre_ref.1, bf16[1024,256]{1,0:T(8,128)(2,1)S(1)} %get-tuple-element.11.near_made_ref), custom_call_target="tpu_custom_call" | custom-call | tf_op jit(solution)/shard_map/spectral/pallas_call | solution.py:504
  41.3 17.7 %all_to_all.10.near_values_ref = bf16[128,16,128]{2,1,0:T(8,128)(2,1)S(1)} all-to-all(bf16[128,16,128]{2,1,0:T(8,128)(2,1)S(1)} %spectral.1), channel_id=1, replica_groups={{58,38,18,114,13,119,33,109,9,44,22,67,116,77,121,8,101,6,104,96,93,75,..., dimensions={0} | all-to-all | bytes 1048576 | tf_op jit(solution)/shard_map/all_to_all | solution.py:526
  59.0 0.0 copy-done.1
  59.0 0.0 copy-done.2
  59.0 0.0 copy-done.3
  59.0 6.3 %synthesis.1 = bf16[2,64,64,128]{3,2,1,0:T(8,128)(2,1)} custom-call(s32[64]{0:T(128)S(1)} %copy-done.3, s32[1,256]{1,0:T(1,128)S(1)} %bitcast.14, bf16[128,16,128]{2,1,0:T(8,128)(2,1)S(1)} %all_to_all.10.near_values_ref, bf16[24,512,256]{2,1,0:T(8,128)(2,1)} %get-tuple-element.12.far_table_ref, f32[15,64,256]{2,1,0:T(8,128)S(1)} %copy-done.1), custom_call_target="tpu_custom_call" | custom-call | tf_op jit(solution)/shard_map/synthesis/pallas_call | solution.py:528
Async XLA Ops:
  9.6 27.6 %all-to-all-start = ((bf16[128,24,128]{2,1,0:T(8,128)(2,1)}), bf16[128,24,128]{2,1,0:T(8,128)(2,1)S(1)}, u32[]{:S(2)}, u32[]{:S(2)}) async-start(bf16[128,24,128]{2,1,0:T(8,128)(2,1)} %get-tuple-element.9), calls=%async_computation | async-start | bytes 1572864 | tf_op jit(solution)/shard_map/all_to_all | solution.py:481
  22.0 1.2 %copy-start = (f32[15,64,256]{2,1,0:T(8,128)S(1)}, f32[15,64,256]{2,1,0:T(8,128)}, u32[]{:S(2)}) copy-start(f32[15,64,256]{2,1,0:T(8,128)} %get-tuple-element.10.step_ref.near_turns_ref) | copy-start | bytes 2949124
  23.2 0.7 %copy-start.4 = (bf16[64,64]{1,0:T(8,128)(2,1)S(1)}, bf16[64,64]{1,0:T(8,128)(2,1)}, u32[]{:S(2)}) copy-start(bf16[64,64]{1,0:T(8,128)(2,1)} %vertical_ref.1) | copy-start | bytes 24580
  37.3 21.7 %copy-start.1 = (f32[15,64,256]{2,1,0:T(8,128)S(1)}, f32[15,64,256]{2,1,0:T(8,128)}, u32[]{:S(2)}) copy-start(f32[15,64,256]{2,1,0:T(8,128)} %get-tuple-element.10.step_ref.near_turns_ref) | copy-start | bytes 2949124
  37.3 21.7 %copy-start.2 = (s32[256]{0:T(256)S(1)}, s32[256]{0:T(256)}, u32[]{:S(2)}) copy-start(s32[256]{0:T(256)} %param.10) | copy-start | bytes 3076
  37.3 21.7 %copy-start.3 = (s32[64]{0:T(128)S(1)}, s32[64]{0:T(128)}, u32[]{:S(2)}) copy-start(s32[64]{0:T(128)} %points_ref.3) | copy-start | bytes 772

commit v4 on v1

--- a/solution.py
+++ b/solution.py
@@ -10,7 +10,7 @@
 
 ROWS = 8
 CHUNK = 128
-BUILT = 3
+BUILT = 2
 VMEM_LIMIT = 56 * 1024 * 1024
 
 SIN_TERMS = (3.141592640130707, -5.167710083507862, 2.550077523214134, -0.5982912856178576, 0.0776576603009221)
@@ -223,7 +223,20 @@
     parting_ref[...] = jnp.where(degree == 2 * (lane % 128) + lane // 128, 1.0, 0.0).astype(jnp.bfloat16)
 
 
-def table_kernel(step_ref, vertical_ref, out_ref, made_ref, pairs_ref, table_ref, sems):
+def legendre_copies(legendre_ref, place_ref, own_ref, sems):
+    return {
+        (slot, q): pltpu.make_async_copy(
+            legendre_ref.at[place_ref[0] + slot, q], own_ref.at[slot, q], sems.at[slot, q]
+        )
+        for slot in range(2) for q in range(2)
+    }
+
+
+def table_kernel(place_ref, step_ref, vertical_ref, legendre_ref, out_ref, made_ref, flipped_ref,
+                 pairs_ref, table_ref, own_ref, sems, own_sems):
+    copies = legendre_copies(legendre_ref, place_ref, own_ref, own_sems)
+    for copy in copies.values():
+        copy.start()
     groups = step_ref.shape[1] // ROWS - BUILT
 
     def departure(g):
@@ -240,6 +253,9 @@
 
     lax.fori_loop(0, groups, group, 0)
     place_matrices(vertical_ref, *matrices_of(made_ref))
+    for (slot, q), copy in copies.items():
+        copy.wait()
+        flipped_ref[slot, q] = own_ref[slot, q].T
     for g in range(groups):
         departure(g).wait()
 
@@ -335,16 +351,16 @@
     )
 
 
-def spectral_kernel(order, place_ref, values_ref, legendre_ref, made_ref, out_ref,
-                    mixed_ref, back_ref, own_ref, sems):
+def spectral_kernel(order, place_ref, values_ref, legendre_ref, made_ref, near_flipped_ref, out_ref,
+                    mixed_ref, back_ref, own_ref, flipped_ref, sems, flipped_sems):
     levels = made_ref.shape[1] // 4
-    copies = {}
-    for slot in range(2):
-        for q in range(2):
-            copies[slot, q] = pltpu.make_async_copy(
-                legendre_ref.at[place_ref[0] + slot, q], own_ref.at[slot, q], sems.at[slot, q]
-            )
-            copies[slot, q].start()
+    copies = legendre_copies(legendre_ref, place_ref, own_ref, sems)
+    flips = {
+        at: pltpu.make_async_copy(near_flipped_ref.at[at], flipped_ref.at[at], flipped_sems.at[at]) for at in copies
+    }
+    for at in copies:
+        flips[at].start()
+        copies[at].start()
     mix_in, mix_out, parting = (part[...] for part in matrices_of(made_ref))
     where = {t: n for n, t in enumerate(order)}
     for p in range(4):
@@ -371,13 +387,15 @@
         parity = place_ref[1 + slot]
         for q in range(2):
             s = (q + parity) % 2
-            copies[slot, q].wait()
-            values = own_ref[slot, q]
-            coefficient = times_transposed(mixed_ref[2 * slot + s], values)
+            flips[slot, q].wait()
+            coefficient = jnp.dot(
+                mixed_ref[2 * slot + s], flipped_ref[slot, q], preferred_element_type=jnp.float32
+            )
             spread = spreads[q]
             scaled = coefficient * jnp.concatenate([spread, spread], axis=0)
+            copies[slot, q].wait()
             back_ref[2 * slot + s] = jnp.dot(
-                scaled.astype(jnp.bfloat16), values, preferred_element_type=jnp.float32
+                scaled.astype(jnp.bfloat16), own_ref[slot, q], preferred_element_type=jnp.float32
             )
     for p in range(4):
         lanes = slice(p * 128, (p + 1) * 128)
@@ -460,43 +478,53 @@
 
     phasors_spec = pl.BlockSpec((15, band_rows, slots), lambda g, *_: (0, 0, 0))
     table_shape = (band_rows // 2 - BUILT * (ROWS // 2), 2 * slots, 2 * CHUNK)
-    table, made = pl.pallas_call(
+    own_shape = (2, 2, half_degree, rows)
+    flipped_shape = (2, 2, rows, half_degree)
+    table, made, flipped = pl.pallas_call(
         table_kernel,
-        grid=(1,),
-        in_specs=[phasors_spec, matrix_spec((levels, levels))],
-        out_specs=[far, matrix_spec(made_shape)],
-        scratch_shapes=[
-            pltpu.VMEM(table_shape, jnp.bfloat16),
-            pltpu.VMEM((ROWS, CHUNK, 2 * slots), jnp.bfloat16),
-            pltpu.SemaphoreType.DMA((band_rows // ROWS - BUILT,)),
-        ],
+        grid_spec=pltpu.PrefetchScalarGridSpec(
+            num_scalar_prefetch=1,
+            grid=(1,),
+            in_specs=[phasors_spec, matrix_spec((levels, levels)), far],
+            out_specs=[far, matrix_spec(made_shape), pl.BlockSpec(flipped_shape, lambda g, *_: (0, 0, 0, 0))],
+            scratch_shapes=[
+                pltpu.VMEM(table_shape, jnp.bfloat16),
+                pltpu.VMEM((ROWS, CHUNK, 2 * slots), jnp.bfloat16),
+                pltpu.VMEM(own_shape, jnp.bfloat16),
+                pltpu.SemaphoreType.DMA((band_rows // ROWS - BUILT,)),
+                pltpu.SemaphoreType.DMA((2, 2)),
+            ],
+        ),
         out_shape=[
             jax.ShapeDtypeStruct(table_shape, jnp.bfloat16),
             jax.ShapeDtypeStruct(made_shape, jnp.bfloat16),
+            jax.ShapeDtypeStruct(flipped_shape, jnp.bfloat16),
         ],
         compiler_params=pltpu.CompilerParams(vmem_limit_bytes=50 * 1024 * 1024),
         cost_estimate=pl.CostEstimate(flops=8 * 10**9, bytes_accessed=9 * 10**6, transcendentals=0),
         name="tables",
-    )(phasors, vertical)
+    )(place, phasors, vertical, legendre)
 
     remixed = pl.pallas_call(
         functools.partial(spectral_kernel, order),
         grid_spec=pltpu.PrefetchScalarGridSpec(
             num_scalar_prefetch=1,
             grid=(1,),
-            in_specs=[blocks_spec(24), far, matrix_spec(made_shape)],
+            in_specs=[blocks_spec(24), far, matrix_spec(made_shape), pl.BlockSpec(memory_space=pl.ANY)],
             out_specs=blocks_spec(16),
             scratch_shapes=[
                 pltpu.VMEM((4, 2 * levels, rows), jnp.bfloat16),
                 pltpu.VMEM((4, 2 * levels, rows), jnp.float32),
-                pltpu.VMEM((2, 2, half_degree, rows), jnp.bfloat16),
+                pltpu.VMEM(own_shape, jnp.bfloat16),
+                pltpu.VMEM(flipped_shape, jnp.bfloat16),
+                pltpu.SemaphoreType.DMA((2, 2)),
                 pltpu.SemaphoreType.DMA((2, 2)),
             ],
         ),
         out_shape=jax.ShapeDtypeStruct((slots // 2, 16, 128), jnp.bfloat16),
         compiler_params=pltpu.CompilerParams(vmem_limit_bytes=50 * 1024 * 1024),
         name="spectral",
-    )(place, arrived, legendre, made)
+    )(place, arrived, legendre, made, flipped)
 
     returned = exchange(remixed)
 

time: 65.6 us -> 65.4 us (level)
  Pallas kernels: 22.6 us -> 23.6 us
  local copies, waits for them, and re-layouts: 1.93 us -> 1.22 us
  other arithmetic: 0.84 us -> 0.16 us
    pallas_call x1, Pallas kernels: 2.81 us -> 3.91 us  [local(): pl.pallas_call(table_kernel, grid_spec=pltpu.PrefetchScalarGridSpec(num_s...]
    unnamed x10, local copies, waits for them, and re-layouts: 1.93 us -> 1.22 us
    select_n x1, other arithmetic: 0.76 us -> 0.08 us  [local(): lax.dynamic_slice_in_dim(owners, 2 * (wave * lax.axis_size('lat') + lat),...]
  transfers between devices with their start and end apart: 1 -> 1, of which waited for: 1 -> 1; matrix products, arithmetic and copies ran while one was open for 1% -> 0% of each run, Pallas kernels for 4% -> 6%
where the time goes in v4:
time: 65.4 us; the launch traced here: 65.1 us
  Pallas kernels  23.6 us (36%)
  blocking collectives  17.7 us (27%)
  starting transfers between devices  11.5 us (18%)
  waiting for transfers between devices  10.8 us (17%)
  local copies, waits for them, and re-layouts  1.22 us (2%)
    all_to_all x1, blocking collectives, local(): returned = exchange(remixed)  17.7 us
    all_to_all x1, starting transfers between devices, local(): arrived = exchange(sums)  11.5 us
    all_to_all x1, waiting for transfers between devices, local(): arrived = exchange(sums)  10.8 us
    pallas_call x1, Pallas kernels, local(): pl.pallas_call(functools.partial(analysis_kernel, order), grid_spec=pltpu...  9.83 us
    pallas_call x1, Pallas kernels, local(): pl.pallas_call(functools.partial(synthesis_kernel, order), grid_spec=pltp...  6.08 us
    pallas_call x1, Pallas kernels, local(): pl.pallas_call(table_kernel, grid_spec=pltpu.PrefetchScalarGridSpec(num_s...  3.91 us
    pallas_call x1, Pallas kernels, local(): pl.pallas_call(functools.partial(spectral_kernel, order), grid_spec=pltpu...  3.77 us
  transfers between devices with their start and end apart: 1, of which 1 were waited for; matrix products, arithmetic and copies ran while one was open for 0% of the time, Pallas kernels for 6%

profile of v4, /device:TPU:1, one launch (start us, length us, event | category | flops | bytes accessed | tf_op | source)
XLA Modules:
  0.0 65.1 jit_solution(1764556875295708330)
XLA Ops:
  0.0 0.0 copy-start.2
  0.0 0.0 copy-start.4
  0.0 9.8 %analysis.1 = (bf16[128,24,128]{2,1,0:T(8,128)(2,1)}, f32[15,64,256]{2,1,0:T(8,128)}) custom-call(s32[64]{0:T(128)} %points_ref.3, f32[64]{0:T(128)} %weights_ref.1, s32[1]{0:T(128)} %bitcast.2.wave_ref, s32[1,256]{1,0:T(1,128)} %bitcast.13, f32[8,1024]{1,0:T(8,128)} %variance_ref.1, bf16[2,64,64,128]{3,2,1,0:T(8,128)(2,1)} %bitcast.15), custom_call_target="tpu_custom_call" | custom-call | tf_op jit(solution)/shard_map/analysis/pallas_call | solution.py:448
  9.8 11.5 %all-to-all-start = ((bf16[128,24,128]{2,1,0:T(8,128)(2,1)}), bf16[128,24,128]{2,1,0:T(8,128)(2,1)S(1)}, u32[]{:S(2)}, u32[]{:S(2)}) async-start(bf16[128,24,128]{2,1,0:T(8,128)(2,1)} %get-tuple-element.10), calls=%async_computation | async-start | bytes 1572864 | tf_op jit(solution)/shard_map/all_to_all | solution.py:477
  21.4 0.0 copy-done.2
  21.4 0.1 and_select_fusion
  21.5 0.1 pad_add_fusion.place_ref
  21.5 0.0 copy-done.4
  21.5 0.0 copy-start
  21.5 1.2 %copy-done = f32[15,64,256]{2,1,0:T(8,128)S(1)} copy-done((f32[15,64,256]{2,1,0:T(8,128)S(1)}, f32[15,64,256]{2,1,0:T(8,128)}, u32[]{:S(2)}) %copy-start) | copy-done | bytes 983064
  22.7 3.9 %tables.1 = (bf16[24,512,256]{2,1,0:T(8,128)(2,1)}, bf16[1024,256]{1,0:T(8,128)(2,1)S(1)}, bf16[2,2,512,512]{3,2,1,0:T(8,128)(2,1)S(1)}) custom-call(s32[3]{0:T(128)S(1)} %pad_add_fusion.place_ref, f32[15,64,256]{2,1,0:T(8,128)S(1)} %copy-done, bf16[64,64]{1,0:T(8,128)(2,1)S(1)} %copy-done.4, bf16[16,2,512,512]{3,2,1,0:T(8,128)(2,1)} %legendre_ref.3), custom_call_target="tpu_custom_call" | custom-call | flops 8000000000 | bytes 9000000 | tf_op jit(solution)/shard_map/tables/pallas_call | solution.py:483
  26.7 10.8 %all-to-all-done.values_ref = bf16[128,24,128]{2,1,0:T(8,128)(2,1)S(1)} async-done(((bf16[128,24,128]{2,1,0:T(8,128)(2,1)}), bf16[128,24,128]{2,1,0:T(8,128)(2,1)S(1)}, u32[]{:S(2)}, u32[]{:S(2)}) %all-to-all-start) | async-done | bytes 786464 | tf_op jit(solution)/shard_map/all_to_all | solution.py:477
  37.5 0.0 copy-start.1
  37.5 0.0 copy-start.3
  37.5 3.8 %spectral.1 = bf16[128,16,128]{2,1,0:T(8,128)(2,1)S(1)} custom-call(s32[3]{0:T(128)S(1)} %pad_add_fusion.place_ref, bf16[128,24,128]{2,1,0:T(8,128)(2,1)S(1)} %all-to-all-done.values_ref, bf16[16,2,512,512]{3,2,1,0:T(8,128)(2,1)} %legendre_ref.3, bf16[1024,256]{1,0:T(8,128)(2,1)S(1)} %get-tuple-element.12.made_ref, ...), custom_call_target="tpu_custom_call" | custom-call | tf_op jit(solution)/shard_map/spectral/pallas_call | solution.py:508
  41.3 17.7 %all_to_all.10.values_ref = bf16[128,16,128]{2,1,0:T(8,128)(2,1)S(1)} all-to-all(bf16[128,16,128]{2,1,0:T(8,128)(2,1)S(1)} %spectral.1), channel_id=1, replica_groups={{58,38,18,114,13,119,33,109,9,44,22,67,116,77,121,8,101,6,104,96,93,75,..., dimensions={0} | all-to-all | bytes 1048576 | tf_op jit(solution)/shard_map/all_to_all | solution.py:529
  59.0 0.0 copy-done.1
  59.0 0.0 copy-done.3
  59.0 6.1 %synthesis.1 = bf16[2,64,64,128]{3,2,1,0:T(8,128)(2,1)} custom-call(s32[64]{0:T(128)S(1)} %copy-done.3, s32[1,256]{1,0:T(1,128)S(1)} %bitcast.14, bf16[128,16,128]{2,1,0:T(8,128)(2,1)S(1)} %all_to_all.10.values_ref, bf16[24,512,256]{2,1,0:T(8,128)(2,1)} %get-tuple-element.14.far_table_ref, f32[15,64,256]{2,1,0:T(8,128)S(1)} %copy-done.1), custom_call_target="tpu_custom_call" | custom-call | tf_op jit(solution)/shard_map/synthesis/pallas_call | solution.py:531
Async XLA Ops:
  0.0 21.4 %copy-start.2 = (s32[256]{0:T(256)S(1)}, s32[256]{0:T(256)}, u32[]{:S(2)}) copy-start(s32[256]{0:T(256)} %param.10) | copy-start | bytes 3076
  0.0 21.5 %copy-start.4 = (bf16[64,64]{1,0:T(8,128)(2,1)S(1)}, bf16[64,64]{1,0:T(8,128)(2,1)}, u32[]{:S(2)}) copy-start(bf16[64,64]{1,0:T(8,128)(2,1)} %vertical_ref.1) | copy-start | bytes 24580
  9.8 27.7 %all-to-all-start = ((bf16[128,24,128]{2,1,0:T(8,128)(2,1)}), bf16[128,24,128]{2,1,0:T(8,128)(2,1)S(1)}, u32[]{:S(2)}, u32[]{:S(2)}) async-start(bf16[128,24,128]{2,1,0:T(8,128)(2,1)} %get-tuple-element.10), calls=%async_computation | async-start | bytes 1572864 | tf_op jit(solution)/shard_map/all_to_all | solution.py:477
  21.5 1.2 %copy-start = (f32[15,64,256]{2,1,0:T(8,128)S(1)}, f32[15,64,256]{2,1,0:T(8,128)}, u32[]{:S(2)}) copy-start(f32[15,64,256]{2,1,0:T(8,128)} %get-tuple-element.11.step_ref.turns_ref) | copy-start | bytes 2949124
  37.5 21.5 %copy-start.1 = (f32[15,64,256]{2,1,0:T(8,128)S(1)}, f32[15,64,256]{2,1,0:T(8,128)}, u32[]{:S(2)}) copy-start(f32[15,64,256]{2,1,0:T(8,128)} %get-tuple-element.11.step_ref.turns_ref) | copy-start | bytes 2949124
  37.5 21.5 %copy-start.3 = (s32[64]{0:T(128)S(1)}, s32[64]{0:T(128)}, u32[]{:S(2)}) copy-start(s32[64]{0:T(128)} %points_ref.3) | copy-start | bytes 772

commit v5 on v1

--- a/solution.py
+++ b/solution.py
@@ -10,7 +10,7 @@
 
 ROWS = 8
 CHUNK = 128
-BUILT = 3
+NEAR = 2
 VMEM_LIMIT = 56 * 1024 * 1024
 
 SIN_TERMS = (3.141592640130707, -5.167710083507862, 2.550077523214134, -0.5982912856178576, 0.0776576603009221)
@@ -223,43 +223,48 @@
     parting_ref[...] = jnp.where(degree == 2 * (lane % 128) + lane // 128, 1.0, 0.0).astype(jnp.bfloat16)
 
 
-def table_kernel(step_ref, vertical_ref, out_ref, made_ref, pairs_ref, table_ref, sems):
-    groups = step_ref.shape[1] // ROWS - BUILT
+def table_kernel(step_ref, vertical_ref, out_ref, near_ref, made_ref, pairs_ref, table_ref, sems):
+    groups = step_ref.shape[1] // ROWS - NEAR
 
     def departure(g):
         at = pl.ds(g * (ROWS // 2), ROWS // 2)
         return pltpu.make_async_copy(pairs_ref.at[at], out_ref.at[at], sems.at[g])
 
-    def group(g, _):
-        here = step_ref.at[:, pl.ds(pl.multiple_of((g + BUILT) * ROWS, ROWS), ROWS)]
+    def group(g, to_ref, at):
+        here = step_ref.at[:, pl.ds(pl.multiple_of(g * ROWS, ROWS), ROWS)]
         for r in range(ROWS):
             build_table(table_ref.at[r], here, r)
-            pairs_ref[g * (ROWS // 2) + r // 2, :, (r % 2) * CHUNK:(r % 2 + 1) * CHUNK] = table_ref[r].T
+            to_ref[at * (ROWS // 2) + r // 2, :, (r % 2) * CHUNK:(r % 2 + 1) * CHUNK] = table_ref[r].T
+
+    def far_group(g, _):
+        group(g + NEAR, pairs_ref, g)
         departure(g).start()
         return 0
 
-    lax.fori_loop(0, groups, group, 0)
+    lax.fori_loop(0, groups, far_group, 0)
+    lax.fori_loop(0, NEAR, lambda g, _: (group(g, near_ref, g), 0)[1], 0)
     place_matrices(vertical_ref, *matrices_of(made_ref))
     for g in range(groups):
         departure(g).wait()
 
 
-def synthesis_kernel(order, points_ref, owners_ref, values_ref, far_table_ref, turns_ref, out_ref,
-                     own_ref, table_ref, built_ref, order_ref, coefs_ref, table_sems, sems):
+def synthesis_kernel(order, points_ref, owners_ref, values_ref, far_table_ref, near_table_ref, turns_ref, out_ref,
+                     own_ref, table_ref, order_ref, coefs_ref, table_sems, sems):
     slots = owners_ref.shape[1]
     tiles = [slice(t, t + 128) for t in range(0, slots, 128)]
     rows, height = own_ref.shape[1:3]
 
-    def arrival(g):
-        at = pl.ds(g * (ROWS // 2), ROWS // 2)
-        return pltpu.make_async_copy(far_table_ref.at[at], table_ref.at[at], table_sems.at[g])
+    def arrival(g, near):
+        to = table_ref.at[pl.ds(g * (ROWS // 2), ROWS // 2)]
+        at = pl.ds((g if near else g - NEAR) * (ROWS // 2), ROWS // 2)
+        return pltpu.make_async_copy((near_table_ref if near else far_table_ref).at[at], to, table_sems.at[g])
 
     def departure(g):
         at = pl.ds(g * ROWS, ROWS)
         return pltpu.make_async_copy(own_ref.at[:, at], out_ref.at[:, at], sems.at[g])
 
-    for g in range(rows // ROWS - BUILT):
-        arrival(g).start()
+    for g in range(rows // ROWS):
+        arrival(g, g < NEAR).start()
     where = {t: n for n, t in enumerate(order)}
     for slot in range(0, slots, 8):
         parts = []
@@ -281,12 +286,9 @@
     position = lax.broadcasted_iota(jnp.int32, (height, CHUNK), 0) // 4 * CHUNK
     position = position + lax.broadcasted_iota(jnp.int32, (height, CHUNK), 1)
 
-    def group(g, built):
+    def group(g, near):
         first = g * ROWS
-        if built:
-            here = turns_ref.at[:, pl.ds(pl.multiple_of(first, ROWS), ROWS)]
-        else:
-            arrival(g - BUILT).wait()
+        arrival(g, near).wait()
         for r in range(ROWS):
             row = first + r
             length = points_ref[row]
@@ -309,20 +311,16 @@
                     before, value = value, tuple(twice * value[c] - before[c] for c in range(2))
                     turned.append(jnp.concatenate(value, axis=1))
             turned = jnp.concatenate(turned, axis=0).astype(jnp.bfloat16)
-            if built:
-                build_table(built_ref.at[r], here, r)
-                gridded = times_transposed(turned, built_ref[r])
-            else:
-                table = table_ref[(g - BUILT) * (ROWS // 2) + r // 2, :, (r % 2) * CHUNK:(r % 2 + 1) * CHUNK]
-                gridded = jnp.dot(turned, table, preferred_element_type=jnp.float32)
+            table = table_ref[g * (ROWS // 2) + r // 2, :, (r % 2) * CHUNK:(r % 2 + 1) * CHUNK]
+            gridded = jnp.dot(turned, table, preferred_element_type=jnp.float32)
             for h in range(2):
                 own_ref[h, row] = jnp.where(
                     position < length, gridded[h * height:(h + 1) * height], 0.0
                 ).astype(jnp.bfloat16)
         departure(g).start()
 
-    for start, end, built in ((0, BUILT, True), (BUILT, rows // ROWS, False)):
-        lax.fori_loop(start, end, lambda g, _, built=built: (group(g, built), 0)[1], 0)
+    for start, end, near in ((0, NEAR, True), (NEAR, rows // ROWS, False)):
+        lax.fori_loop(start, end, lambda g, _, near=near: (group(g, near), 0)[1], 0)
     for g in range(rows // ROWS):
         departure(g).wait()
 
@@ -459,19 +457,21 @@
     arrived = exchange(sums)
 
     phasors_spec = pl.BlockSpec((15, band_rows, slots), lambda g, *_: (0, 0, 0))
-    table_shape = (band_rows // 2 - BUILT * (ROWS // 2), 2 * slots, 2 * CHUNK)
-    table, made = pl.pallas_call(
+    table_shape = (band_rows // 2 - NEAR * (ROWS // 2), 2 * slots, 2 * CHUNK)
+    near_shape = (NEAR * (ROWS // 2), 2 * slots, 2 * CHUNK)
+    table, near_table, made = pl.pallas_call(
         table_kernel,
         grid=(1,),
         in_specs=[phasors_spec, matrix_spec((levels, levels))],
-        out_specs=[far, matrix_spec(made_shape)],
+        out_specs=[far, pl.BlockSpec(near_shape, lambda g, *_: (0, 0, 0)), matrix_spec(made_shape)],
         scratch_shapes=[
             pltpu.VMEM(table_shape, jnp.bfloat16),
             pltpu.VMEM((ROWS, CHUNK, 2 * slots), jnp.bfloat16),
-            pltpu.SemaphoreType.DMA((band_rows // ROWS - BUILT,)),
+            pltpu.SemaphoreType.DMA((band_rows // ROWS - NEAR,)),
         ],
         out_shape=[
             jax.ShapeDtypeStruct(table_shape, jnp.bfloat16),
+            jax.ShapeDtypeStruct(near_shape, jnp.bfloat16),
             jax.ShapeDtypeStruct(made_shape, jnp.bfloat16),
         ],
         compiler_params=pltpu.CompilerParams(vmem_limit_bytes=50 * 1024 * 1024),
@@ -505,22 +505,21 @@
         grid_spec=pltpu.PrefetchScalarGridSpec(
             num_scalar_prefetch=1,
             grid=(1,),
-            in_specs=[own_spec, blocks_spec(16), far, phasors_spec],
+            in_specs=[own_spec, blocks_spec(16), far, pl.BlockSpec(memory_space=pl.ANY), phasors_spec],
             out_specs=far,
             scratch_shapes=[
                 pltpu.VMEM(field.shape, jnp.bfloat16),
-                pltpu.VMEM(table_shape, jnp.bfloat16),
-                pltpu.VMEM((ROWS, CHUNK, 2 * slots), jnp.bfloat16),
+                pltpu.VMEM((band_rows // 2, 2 * slots, 2 * CHUNK), jnp.bfloat16),
                 pltpu.VMEM((slots // 128, 8, 128, 128), jnp.float32),
                 pltpu.VMEM((slots // 128, 128, 8, 128), jnp.float32),
-                pltpu.SemaphoreType.DMA((band_rows // ROWS - BUILT,)),
+                pltpu.SemaphoreType.DMA((band_rows // ROWS,)),
                 pltpu.SemaphoreType.DMA((band_rows // ROWS,)),
             ],
         ),
         out_shape=jax.ShapeDtypeStruct(field.shape, jnp.bfloat16),
         compiler_params=pltpu.CompilerParams(vmem_limit_bytes=50 * 1024 * 1024),
         name="synthesis",
-    )(points, own, returned, table, phasors)
+    )(points, own, returned, table, near_table, phasors)
     smoothed = smoothed.reshape(2, band_rows, chunks, few_levels, CHUNK).transpose(0, 1, 3, 2, 4)
     return smoothed.reshape(grid_field.shape)
 

time: 65.6 us -> 65.4 us (level)
  waiting for transfers between devices: 10.6 us -> 11.5 us
  local copies, waits for them, and re-layouts: 1.93 us -> 1.22 us
  other arithmetic: 0.84 us -> 0.16 us
    all_to_all x1, waiting for transfers between devices: 10.6 us -> 11.5 us  [local(): arrived = exchange(sums)]
    unnamed x10, local copies, waits for them, and re-layouts: 1.93 us -> 1.22 us
    select_n x1, other arithmetic: 0.76 us -> 0.08 us  [local(): lax.dynamic_slice_in_dim(owners, 2 * (wave * lax.axis_size('lat') + lat),...]
  transfers between devices with their start and end apart: 1 -> 1, of which waited for: 1 -> 1; matrix products, arithmetic and copies ran while one was open for 1% -> 0% of each run, Pallas kernels for 4% -> 5%
where the time goes in v5:
time: 65.4 us; the launch traced here: 65.1 us
  Pallas kernels  22.9 us (35%)
  blocking collectives  17.7 us (27%)
  starting transfers between devices  11.5 us (18%)
  waiting for transfers between devices  11.5 us (18%)
  local copies, waits for them, and re-layouts  1.22 us (2%)
    all_to_all x1, blocking collectives, local(): returned = exchange(remixed)  17.7 us
    all_to_all x1, starting transfers between devices, local(): arrived = exchange(sums)  11.5 us
    all_to_all x1, waiting for transfers between devices, local(): arrived = exchange(sums)  11.5 us
    pallas_call x1, Pallas kernels, local(): pl.pallas_call(functools.partial(analysis_kernel, order), grid_spec=pltpu...  9.83 us
    pallas_call x1, Pallas kernels, local(): pl.pallas_call(functools.partial(synthesis_kernel, order), grid_spec=pltp...  5.83 us
    pallas_call x1, Pallas kernels, local(): pl.pallas_call(functools.partial(spectral_kernel, order), grid_spec=pltpu...  3.98 us
    pallas_call x1, Pallas kernels, local(): pl.pallas_call(table_kernel, grid=(1,), in_specs=[phasors_spec, matrix_sp...  3.29 us
  transfers between devices with their start and end apart: 1, of which 1 were waited for; matrix products, arithmetic and copies ran while one was open for 0% of the time, Pallas kernels for 5%

profile of v5, /device:TPU:1, one launch (start us, length us, event | category | flops | bytes accessed | tf_op | source)
XLA Modules:
  0.0 65.1 jit_solution(4382146982199391030)
XLA Ops:
  0.0 0.0 copy-start.2
  0.0 0.0 copy-start.4
  0.0 9.8 %analysis.1 = (bf16[128,24,128]{2,1,0:T(8,128)(2,1)}, f32[15,64,256]{2,1,0:T(8,128)}) custom-call(s32[64]{0:T(128)} %points_ref.3, f32[64]{0:T(128)} %weights_ref.1, s32[1]{0:T(128)} %bitcast.2.wave_ref, s32[1,256]{1,0:T(1,128)} %bitcast.13, f32[8,1024]{1,0:T(8,128)} %variance_ref.1, bf16[2,64,64,128]{3,2,1,0:T(8,128)(2,1)} %bitcast.15), custom_call_target="tpu_custom_call" | custom-call | tf_op jit(solution)/shard_map/analysis/pallas_call | solution.py:428
  9.8 11.5 %all-to-all-start = ((bf16[128,24,128]{2,1,0:T(8,128)(2,1)}), bf16[128,24,128]{2,1,0:T(8,128)(2,1)S(1)}, u32[]{:S(2)}, u32[]{:S(2)}) async-start(bf16[128,24,128]{2,1,0:T(8,128)(2,1)} %get-tuple-element.10), calls=%async_computation | async-start | bytes 1572864 | tf_op jit(solution)/shard_map/all_to_all | solution.py:457
  21.4 0.0 copy-done.2
  21.4 0.1 and_select_fusion
  21.5 0.1 pad_add_fusion.place_ref
  21.5 0.0 copy-done.4
  21.5 0.0 copy-start
  21.5 1.2 %copy-done = f32[15,64,256]{2,1,0:T(8,128)S(1)} copy-done((f32[15,64,256]{2,1,0:T(8,128)S(1)}, f32[15,64,256]{2,1,0:T(8,128)}, u32[]{:S(2)}) %copy-start) | copy-done | bytes 983064
  22.7 3.3 %tables.1 = (bf16[24,512,256]{2,1,0:T(8,128)(2,1)}, bf16[8,512,256]{2,1,0:T(8,128)(2,1)S(1)}, bf16[1024,256]{1,0:T(8,128)(2,1)S(1)}) custom-call(f32[15,64,256]{2,1,0:T(8,128)S(1)} %copy-done, bf16[64,64]{1,0:T(8,128)(2,1)S(1)} %copy-done.4), custom_call_target="tpu_custom_call" | custom-call | flops 8000000000 | bytes 9000000 | tf_op jit(solution)/shard_map/tables/pallas_call | solution.py:462
  26.0 11.5 %all-to-all-done.values_ref = bf16[128,24,128]{2,1,0:T(8,128)(2,1)S(1)} async-done(((bf16[128,24,128]{2,1,0:T(8,128)(2,1)}), bf16[128,24,128]{2,1,0:T(8,128)(2,1)S(1)}, u32[]{:S(2)}, u32[]{:S(2)}) %all-to-all-start) | async-done | bytes 786464 | tf_op jit(solution)/shard_map/all_to_all | solution.py:457
  37.5 0.0 copy-start.1
  37.5 0.0 copy-start.3
  37.5 4.0 %spectral.1 = bf16[128,16,128]{2,1,0:T(8,128)(2,1)S(1)} custom-call(s32[3]{0:T(128)S(1)} %pad_add_fusion.place_ref, bf16[128,24,128]{2,1,0:T(8,128)(2,1)S(1)} %all-to-all-done.values_ref, bf16[16,2,512,512]{3,2,1,0:T(8,128)(2,1)} %legendre_ref.1, bf16[1024,256]{1,0:T(8,128)(2,1)S(1)} %get-tuple-element.12.made_ref), custom_call_target="tpu_custom_call" | custom-call | tf_op jit(solution)/shard_map/spectral/pallas_call | solution.py:482
  41.5 17.7 %all_to_all.10.values_ref = bf16[128,16,128]{2,1,0:T(8,128)(2,1)S(1)} all-to-all(bf16[128,16,128]{2,1,0:T(8,128)(2,1)S(1)} %spectral.1), channel_id=1, replica_groups={{58,38,18,114,13,119,33,109,9,44,22,67,116,77,121,8,101,6,104,96,93,75,..., dimensions={0} | all-to-all | bytes 1048576 | tf_op jit(solution)/shard_map/all_to_all | solution.py:501
  59.2 0.0 copy-done.1
  59.2 0.0 copy-done.3
  59.2 5.8 %synthesis.1 = bf16[2,64,64,128]{3,2,1,0:T(8,128)(2,1)} custom-call(s32[64]{0:T(128)S(1)} %copy-done.3, s32[1,256]{1,0:T(1,128)S(1)} %bitcast.14, bf16[128,16,128]{2,1,0:T(8,128)(2,1)S(1)} %all_to_all.10.values_ref, bf16[24,512,256]{2,1,0:T(8,128)(2,1)} %get-tuple-element.13.far_table_ref, bf16[8,512,256]{2,1,0:T(8,128)(2,1)S(1)} %get-tuple-element.14.near_table_ref, ...), custom_call_target="tpu_custom_call" | custom-call | tf_op jit(solution)/shard_map/synthesis/pallas_call | solution.py:503
Async XLA Ops:
  0.0 21.4 %copy-start.2 = (s32[256]{0:T(256)S(1)}, s32[256]{0:T(256)}, u32[]{:S(2)}) copy-start(s32[256]{0:T(256)} %param.10) | copy-start | bytes 3076
  0.0 21.5 %copy-start.4 = (bf16[64,64]{1,0:T(8,128)(2,1)S(1)}, bf16[64,64]{1,0:T(8,128)(2,1)}, u32[]{:S(2)}) copy-start(bf16[64,64]{1,0:T(8,128)(2,1)} %vertical_ref.1) | copy-start | bytes 24580
  9.8 27.7 %all-to-all-start = ((bf16[128,24,128]{2,1,0:T(8,128)(2,1)}), bf16[128,24,128]{2,1,0:T(8,128)(2,1)S(1)}, u32[]{:S(2)}, u32[]{:S(2)}) async-start(bf16[128,24,128]{2,1,0:T(8,128)(2,1)} %get-tuple-element.10), calls=%async_computation | async-start | bytes 1572864 | tf_op jit(solution)/shard_map/all_to_all | solution.py:457
  21.5 1.2 %copy-start = (f32[15,64,256]{2,1,0:T(8,128)S(1)}, f32[15,64,256]{2,1,0:T(8,128)}, u32[]{:S(2)}) copy-start(f32[15,64,256]{2,1,0:T(8,128)} %get-tuple-element.11.step_ref.turns_ref) | copy-start | bytes 2949124
  37.5 21.7 %copy-start.1 = (f32[15,64,256]{2,1,0:T(8,128)S(1)}, f32[15,64,256]{2,1,0:T(8,128)}, u32[]{:S(2)}) copy-start(f32[15,64,256]{2,1,0:T(8,128)} %get-tuple-element.11.step_ref.turns_ref) | copy-start | bytes 2949124
  37.5 21.7 %copy-start.3 = (s32[64]{0:T(128)S(1)}, s32[64]{0:T(128)}, u32[]{:S(2)}) copy-start(s32[64]{0:T(128)} %points_ref.3) | copy-start | bytes 772

commit v6 on v5

--- a/solution.py
+++ b/solution.py
@@ -2,7 +2,6 @@
 
 import jax
 import jax.numpy as jnp
-import numpy as np
 from jax import lax
 from jax.experimental import pallas as pl
 from jax.experimental.pallas import tpu as pltpu
@@ -401,7 +400,7 @@
     place = jnp.concatenate([(2 * lat).reshape(1), parities])
     params = pltpu.CompilerParams(vmem_limit_bytes=VMEM_LIMIT)
 
-    order = [int(t) for t in np.random.RandomState(5).permutation(slots // 2)]
+    order = [37 * t % (slots // 2) for t in range(slots // 2)]
     exchange = functools.partial(
         lax.all_to_all, axis_name=("wave", "lat"), split_axis=0, concat_axis=0, axis_index_groups=[order], tiled=True
     )

time: 65.4 us -> 65.6 us (level)
  no operation moved by 1% of the time
where the time goes in v6:
time: 65.6 us; the launch traced here: 65.3 us
  Pallas kernels  22.9 us (35%)
  blocking collectives  17.4 us (27%)
  waiting for transfers between devices  12 us (18%)
  starting transfers between devices  11.5 us (18%)
  local copies, waits for them, and re-layouts  1.22 us (2%)
    all_to_all x1, blocking collectives, local(): returned = exchange(remixed)  17.4 us
    all_to_all x1, waiting for transfers between devices, local(): arrived = exchange(sums)  12 us
    all_to_all x1, starting transfers between devices, local(): arrived = exchange(sums)  11.5 us
    pallas_call x1, Pallas kernels, local(): pl.pallas_call(functools.partial(analysis_kernel, order), grid_spec=pltpu...  9.82 us
    pallas_call x1, Pallas kernels, local(): pl.pallas_call(functools.partial(synthesis_kernel, order), grid_spec=pltp...  5.82 us
    pallas_call x1, Pallas kernels, local(): pl.pallas_call(functools.partial(spectral_kernel, order), grid_spec=pltpu...  3.99 us
    pallas_call x1, Pallas kernels, local(): pl.pallas_call(table_kernel, grid=(1,), in_specs=[phasors_spec, matrix_sp...  3.29 us
  transfers between devices with their start and end apart: 1, of which 1 were waited for; matrix products, arithmetic and copies ran while one was open for 0% of the time, Pallas kernels for 5%

profile of v6, /device:TPU:1, one launch (start us, length us, event | category | flops | bytes accessed | tf_op | source)
XLA Modules:
  0.0 65.3 jit_solution(11110274364631592123)
XLA Ops:
  0.0 0.0 copy-start.2
  0.0 0.0 copy-start.4
  0.0 9.8 %analysis.1 = (bf16[128,24,128]{2,1,0:T(8,128)(2,1)}, f32[15,64,256]{2,1,0:T(8,128)}) custom-call(s32[64]{0:T(128)} %points_ref.3, f32[64]{0:T(128)} %weights_ref.1, s32[1]{0:T(128)} %bitcast.2.wave_ref, s32[1,256]{1,0:T(1,128)} %bitcast.13, f32[8,1024]{1,0:T(8,128)} %variance_ref.1, bf16[2,64,64,128]{3,2,1,0:T(8,128)(2,1)} %bitcast.15), custom_call_target="tpu_custom_call" | custom-call | tf_op jit(solution)/shard_map/analysis/pallas_call | solution.py:427
  9.8 11.5 %all-to-all-start = ((bf16[128,24,128]{2,1,0:T(8,128)(2,1)}), bf16[128,24,128]{2,1,0:T(8,128)(2,1)S(1)}, u32[]{:S(2)}, u32[]{:S(2)}) async-start(bf16[128,24,128]{2,1,0:T(8,128)(2,1)} %get-tuple-element.10), calls=%async_computation | async-start | bytes 1572864 | tf_op jit(solution)/shard_map/all_to_all | solution.py:456
  21.4 0.0 copy-done.2
  21.4 0.1 and_select_fusion
  21.5 0.1 pad_add_fusion.place_ref
  21.5 0.0 copy-done.4
  21.5 0.0 copy-start
  21.5 1.2 %copy-done = f32[15,64,256]{2,1,0:T(8,128)S(1)} copy-done((f32[15,64,256]{2,1,0:T(8,128)S(1)}, f32[15,64,256]{2,1,0:T(8,128)}, u32[]{:S(2)}) %copy-start) | copy-done | bytes 983064
  22.7 3.3 %tables.1 = (bf16[24,512,256]{2,1,0:T(8,128)(2,1)}, bf16[8,512,256]{2,1,0:T(8,128)(2,1)S(1)}, bf16[1024,256]{1,0:T(8,128)(2,1)S(1)}) custom-call(f32[15,64,256]{2,1,0:T(8,128)S(1)} %copy-done, bf16[64,64]{1,0:T(8,128)(2,1)S(1)} %copy-done.4), custom_call_target="tpu_custom_call" | custom-call | flops 8000000000 | bytes 9000000 | tf_op jit(solution)/shard_map/tables/pallas_call | solution.py:461
  26.0 12.0 %all-to-all-done.values_ref = bf16[128,24,128]{2,1,0:T(8,128)(2,1)S(1)} async-done(((bf16[128,24,128]{2,1,0:T(8,128)(2,1)}), bf16[128,24,128]{2,1,0:T(8,128)(2,1)S(1)}, u32[]{:S(2)}, u32[]{:S(2)}) %all-to-all-start) | async-done | bytes 786464 | tf_op jit(solution)/shard_map/all_to_all | solution.py:456
  38.0 0.0 copy-start.1
  38.0 0.0 copy-start.3
  38.0 4.0 %spectral.1 = bf16[128,16,128]{2,1,0:T(8,128)(2,1)S(1)} custom-call(s32[3]{0:T(128)S(1)} %pad_add_fusion.place_ref, bf16[128,24,128]{2,1,0:T(8,128)(2,1)S(1)} %all-to-all-done.values_ref, bf16[16,2,512,512]{3,2,1,0:T(8,128)(2,1)} %legendre_ref.1, bf16[1024,256]{1,0:T(8,128)(2,1)S(1)} %get-tuple-element.12.made_ref), custom_call_target="tpu_custom_call" | custom-call | tf_op jit(solution)/shard_map/spectral/pallas_call | solution.py:481
  42.0 17.4 %all_to_all.10.values_ref = bf16[128,16,128]{2,1,0:T(8,128)(2,1)S(1)} all-to-all(bf16[128,16,128]{2,1,0:T(8,128)(2,1)S(1)} %spectral.1), channel_id=1, replica_groups={{0,84,41,125,66,23,107,48,5,89,46,114,71,28,96,53,10,94,35,119,76,17,10..., dimensions={0} | all-to-all | bytes 1048576 | tf_op jit(solution)/shard_map/all_to_all | solution.py:500
  59.4 0.0 copy-done.1
  59.4 0.0 copy-done.3
  59.4 5.8 %synthesis.1 = bf16[2,64,64,128]{3,2,1,0:T(8,128)(2,1)} custom-call(s32[64]{0:T(128)S(1)} %copy-done.3, s32[1,256]{1,0:T(1,128)S(1)} %bitcast.14, bf16[128,16,128]{2,1,0:T(8,128)(2,1)S(1)} %all_to_all.10.values_ref, bf16[24,512,256]{2,1,0:T(8,128)(2,1)} %get-tuple-element.13.far_table_ref, bf16[8,512,256]{2,1,0:T(8,128)(2,1)S(1)} %get-tuple-element.14.near_table_ref, ...), custom_call_target="tpu_custom_call" | custom-call | tf_op jit(solution)/shard_map/synthesis/pallas_call | solution.py:502
Async XLA Ops:
  0.0 21.4 %copy-start.2 = (s32[256]{0:T(256)S(1)}, s32[256]{0:T(256)}, u32[]{:S(2)}) copy-start(s32[256]{0:T(256)} %param.10) | copy-start | bytes 3076
  0.0 21.5 %copy-start.4 = (bf16[64,64]{1,0:T(8,128)(2,1)S(1)}, bf16[64,64]{1,0:T(8,128)(2,1)}, u32[]{:S(2)}) copy-start(bf16[64,64]{1,0:T(8,128)(2,1)} %vertical_ref.1) | copy-start | bytes 24580
  9.8 28.2 %all-to-all-start = ((bf16[128,24,128]{2,1,0:T(8,128)(2,1)}), bf16[128,24,128]{2,1,0:T(8,128)(2,1)S(1)}, u32[]{:S(2)}, u32[]{:S(2)}) async-start(bf16[128,24,128]{2,1,0:T(8,128)(2,1)} %get-tuple-element.10), calls=%async_computation | async-start | bytes 1572864 | tf_op jit(solution)/shard_map/all_to_all | solution.py:456
  21.5 1.2 %copy-start = (f32[15,64,256]{2,1,0:T(8,128)S(1)}, f32[15,64,256]{2,1,0:T(8,128)}, u32[]{:S(2)}) copy-start(f32[15,64,256]{2,1,0:T(8,128)} %get-tuple-element.11.step_ref.turns_ref) | copy-start | bytes 2949124
  38.0 21.5 %copy-start.1 = (f32[15,64,256]{2,1,0:T(8,128)S(1)}, f32[15,64,256]{2,1,0:T(8,128)}, u32[]{:S(2)}) copy-start(f32[15,64,256]{2,1,0:T(8,128)} %get-tuple-element.11.step_ref.turns_ref) | copy-start | bytes 2949124
  38.0 21.5 %copy-start.3 = (s32[64]{0:T(128)S(1)}, s32[64]{0:T(128)}, u32[]{:S(2)}) copy-start(s32[64]{0:T(128)} %points_ref.3) | copy-start | bytes 772
